TPU v7x, 32 devices: a whole 2x2x4 slice. The times are simulated.
32 devices in a mesh: expert: 8 (over y, x, core), fsdp: 4 (over z).
Axes of the slice: x: 2, y: 2, z: 4, core: 2. Of those that a mesh axis runs over, the one named last changes fastest.
Arguments:
- tokens: bfloat16 [4096, 2048], P(('expert', 'fsdp')), may hold values from -6 to 6
- lengths: int32 [32, 4], P(('expert', 'fsdp')), may hold values from 1 to 96, 128 in all within a row
- routes: int32 [4096, 8], P(('expert', 'fsdp')), may hold values from 0 to 15, all different within a row; in each aligned block of 128 rows (0 to 127, 128 to 255, ...) at most 96 rows name the same one
- attn_gain: bfloat16 [2048], P('fsdp'), may hold values from 0.25 to 1.75
- w_query: bfloat16 [2048, 4096], P('fsdp'), may hold values from -0.125 to 0.125
- key_projection: bfloat16 [2048, 512], P('fsdp'), may hold values from -0.125 to 0.125
- value_projection: bfloat16 [2048, 512], P('fsdp'), may hold values from -0.125 to 0.125
- w_out: bfloat16 [4096, 2048], P('fsdp'), may hold values from -0.375 to 0.375
- query_gain: bfloat16 [128], P('fsdp'), may hold values from 0.25 to 1.75
- key_gain: bfloat16 [128], P('fsdp'), may hold values from 0.25 to 1.75
- ffn_gain: bfloat16 [2048], P('fsdp'), may hold values from 0.25 to 1.75
- w_router: bfloat16 [2048, 16], P('fsdp'), may hold values from -0.0625 to 0.0625
- w_gate: bfloat16 [16, 2048, 768], P('expert', None, 'fsdp'), may hold values from -0.125 to 0.125
- w_up: bfloat16 [16, 2048, 768], P('expert', None, 'fsdp'), may hold values from -0.125 to 0.125
- w_down: bfloat16 [16, 768, 2048], P('expert', 'fsdp'), may hold values from -0.625 to 0.625
- cotangent: bfloat16 [4096, 2048], P(('expert', 'fsdp')), may hold values from -6 to 6
Outputs:
- block_out: bfloat16 [4096, 2048], P(('expert', 'fsdp'))
- grad_tokens: float32 [4096, 2048], P(('expert', 'fsdp'))
- grad_attn_gain: float32 [2048], P('fsdp')
- grad_w_query: float32 [2048, 4096], P('fsdp')
- grad_w_key: float32 [2048, 512], P('fsdp')
- grad_w_value: float32 [2048, 512], P('fsdp')
- grad_w_out: float32 [4096, 2048], P('fsdp')
- grad_query_gain: float32 [128], P('fsdp')
- grad_key_gain: float32 [128], P('fsdp')
- grad_ffn_gain: float32 [2048], P('fsdp')
- grad_w_router: float32 [2048, 16], P('fsdp')
- grad_w_gate: float32 [16, 2048, 768], P('expert', None, 'fsdp')
- grad_w_up: float32 [16, 2048, 768], P('expert', None, 'fsdp')
- grad_w_down: float32 [16, 768, 2048], P('expert', 'fsdp')
Inputs may be any that keep to these rules, and one draw needn't show every extreme that they name: The lengths of one device sum to 128; each device holds one sequence of exactly 96 tokens. `routes`: A token names 8 different experts. Among the 128 tokens of one device no expert is named more than 96 times, and some expert reaches 96 on some device.
All inputs are finite; a program needn't handle non-finite values.
Results may differ from a plain program's by a relative error of at most 0.024.
Values may be sent and summed in bfloat16 or wider, within the bound.
A program may use at most 448 MiB of HBM per device.

v0:
```python
import jax
import jax.numpy as jnp
from jax import lax
from jax.sharding import PartitionSpec as P

MODEL_WIDTH = 2048
QUERY_HEADS = 32
KEY_VALUE_HEADS = 4
HEAD_WIDTH = 128
TOPK = 8
EXP_DEV = 2
DEVICE_TOKENS = 128
SEQ_SLOTS = 4


epsilon = 1e-06
rope_base = 1000000.0
masked_score = -1e30


def layout(lengths_row, tok_count, slot_count):
    seq_ends = jnp.cumsum(lengths_row)
    starts = seq_ends - lengths_row
    places = jnp.arange(tok_count, dtype=jnp.int32)
    segment = jnp.sum((places[:, None] >= seq_ends[None, :]).astype(jnp.int32), axis=1)
    member = segment[:, None] == jnp.arange(slot_count, dtype=jnp.int32)[None, :]
    start_of = jnp.sum(jnp.where(member, starts[None, :], 0), axis=1)
    return (places - start_of, segment)


def rope_tables(places, head_size):
    frequency = rope_base ** (-jnp.arange(0, head_size, 2, dtype=jnp.float32) / head_size)
    angles = places.astype(jnp.float32)[:, None] * frequency[None, :]
    angles = jnp.concatenate([angles, angles], axis=-1)
    return (jnp.cos(angles)[:, None, :], jnp.sin(angles)[:, None, :])


def rotate(values, cosine, sine_table):
    half_width = values.shape[-1] // 2
    turned = jnp.concatenate([-values[..., half_width:], values[..., :half_width]], axis=-1)
    return values * cosine + turned * sine_table


def unrotate(gradient, cosine, sine_table):
    scaled = gradient * sine_table
    half_width = gradient.shape[-1] // 2
    return gradient * cosine + jnp.concatenate(
        [scaled[..., half_width:], -scaled[..., :half_width]], axis=-1
    )


def norm_back(gradient, unit_value, inverse):
    return inverse * (
        gradient - unit_value * jnp.mean(gradient * unit_value, axis=-1, keepdims=True)
    )


def probabilities_of(query_head_groups, key_low, allowed, score_scale):
    scores = (
        jnp.einsum("qhgd,khd->hgqk", query_head_groups, key_low, preferred_element_type=jnp.float32)
        * score_scale
    )
    scores = jnp.where(allowed, scores, masked_score)
    weights = jnp.exp(scores - jnp.max(scores, axis=-1, keepdims=True))
    return weights / jnp.sum(weights, axis=-1, keepdims=True)


def per_device(
    tokens,
    lengths,
    routes,
    attn_gain,
    w_query,
    key_projection,
    value_projection,
    w_out,
    query_gain,
    key_gain,
    ffn_gain,
    w_router,
    w_gate,
    w_up,
    w_down,
    cotangent,
):
    groups = lax.axis_size("expert")
    experts_all = w_router.shape[1]
    capacity = 3 * DEVICE_TOKENS * TOPK // (2 * experts_all)
    group_width = QUERY_HEADS // KEY_VALUE_HEADS
    score_scale = HEAD_WIDTH ** (-0.5)
    (
        attn_all,
        query_all,
        key_gathered,
        value_all,
        out_all,
        query_gain_all,
        key_gain_all,
        ffn_all,
        router_all,
    ) = (
        lax.all_gather(attn_gain, "fsdp", axis=0, tiled=True),
        lax.all_gather(w_query, "fsdp", axis=0, tiled=True),
        lax.all_gather(key_projection, "fsdp", axis=0, tiled=True),
        lax.all_gather(value_projection, "fsdp", axis=0, tiled=True),
        lax.all_gather(w_out, "fsdp", axis=0, tiled=True),
        lax.all_gather(query_gain, "fsdp", axis=0, tiled=True),
        lax.all_gather(key_gain, "fsdp", axis=0, tiled=True),
        lax.all_gather(ffn_gain, "fsdp", axis=0, tiled=True),
        lax.all_gather(w_router, "fsdp", axis=0, tiled=True),
    )
    attn_gain_f = attn_all.astype(jnp.float32)
    ffn_gain_f = ffn_all.astype(jnp.float32)
    query_gain_f = query_gain_all.astype(jnp.float32)
    key_gain_f = key_gain_all.astype(jnp.float32)
    source = tokens.astype(jnp.float32)
    attn_inverse = lax.rsqrt(jnp.mean(source * source, axis=-1, keepdims=True) + epsilon)
    attn_unit = source * attn_inverse
    normed_input = (attn_unit * attn_gain_f).astype(jnp.bfloat16)
    query_raw = jnp.dot(normed_input, query_all, preferred_element_type=jnp.float32).reshape(
        DEVICE_TOKENS, QUERY_HEADS, HEAD_WIDTH
    )
    key_unrotated = jnp.dot(normed_input, key_gathered, preferred_element_type=jnp.float32).reshape(
        DEVICE_TOKENS, KEY_VALUE_HEADS, HEAD_WIDTH
    )
    value_low = (
        jnp.dot(normed_input, value_all, preferred_element_type=jnp.float32)
        .astype(jnp.bfloat16)
        .reshape(DEVICE_TOKENS, KEY_VALUE_HEADS, HEAD_WIDTH)
    )
    places, segment_ids = layout(lengths[0], DEVICE_TOKENS, SEQ_SLOTS)
    cosine, sine_table = rope_tables(places, HEAD_WIDTH)
    query_inverse = lax.rsqrt(jnp.mean(query_raw * query_raw, axis=-1, keepdims=True) + epsilon)
    query_unit = query_raw * query_inverse
    query_lowered = rotate(query_unit * query_gain_f, cosine, sine_table).astype(jnp.bfloat16)
    key_inverse = lax.rsqrt(
        jnp.mean(key_unrotated * key_unrotated, axis=-1, keepdims=True) + epsilon
    )
    key_unit = key_unrotated * key_inverse
    key_low = rotate(key_unit * key_gain_f, cosine, sine_table).astype(jnp.bfloat16)
    row_ids = jnp.arange(DEVICE_TOKENS, dtype=jnp.int32)
    allowed = (segment_ids[:, None] == segment_ids[None, :]) & (
        row_ids[None, :] <= row_ids[:, None]
    )
    query_head_groups = query_lowered.reshape(
        DEVICE_TOKENS, KEY_VALUE_HEADS, group_width, HEAD_WIDTH
    )
    probabilities = probabilities_of(query_head_groups, key_low, allowed, score_scale)
    attended = jnp.einsum(
        "hgqk,khd->qhgd",
        probabilities.astype(jnp.bfloat16),
        value_low,
        preferred_element_type=jnp.float32,
    )
    mixed_low = attended.reshape(DEVICE_TOKENS, QUERY_HEADS * HEAD_WIDTH).astype(jnp.bfloat16)
    branch = jnp.dot(mixed_low, out_all, preferred_element_type=jnp.float32)
    middle = source + branch
    ffn_inverse = lax.rsqrt(jnp.mean(middle * middle, axis=-1, keepdims=True) + epsilon)
    ffn_unit = middle * ffn_inverse
    second = (ffn_unit * ffn_gain_f).astype(jnp.bfloat16)
    logits = jnp.dot(second, router_all, preferred_element_type=jnp.float32)
    picked = jnp.take_along_axis(logits, routes, axis=1)
    picked = jnp.exp(picked - jnp.max(picked, axis=1, keepdims=True))
    gate_share = picked / jnp.sum(picked, axis=1, keepdims=True)
    pair_count = DEVICE_TOKENS * TOPK
    flat_routes = routes.reshape(pair_count)
    expert_ids = jnp.arange(experts_all, dtype=jnp.int32)
    chosen = (flat_routes[:, None] == expert_ids[None, :]).astype(jnp.int32)
    slot_ranks = jnp.sum(chosen * (jnp.cumsum(chosen, axis=0) - 1), axis=1)
    slot_ids = flat_routes * capacity + slot_ranks
    owner_pair = (
        jnp.full((experts_all * capacity,), pair_count, jnp.int32)
        .at[slot_ids]
        .set(jnp.arange(pair_count, dtype=jnp.int32))
    )
    padded_second = jnp.concatenate([second, jnp.zeros((1, MODEL_WIDTH), jnp.bfloat16)], axis=0)
    outgoing = padded_second[owner_pair // TOPK].reshape(groups, EXP_DEV, capacity, MODEL_WIDTH)
    arrived = lax.all_to_all(outgoing, "expert", split_axis=0, concat_axis=2, tiled=True).reshape(
        EXP_DEV, groups * capacity, MODEL_WIDTH
    )
    group_rows = lax.all_gather(arrived, "fsdp", axis=1, tiled=True)
    gate_act = jnp.einsum("erd,edf->erf", group_rows, w_gate, preferred_element_type=jnp.float32)
    up_act = jnp.einsum("erd,edf->erf", group_rows, w_up, preferred_element_type=jnp.float32)
    hidden_low = (jax.nn.silu(gate_act) * up_act).astype(jnp.bfloat16)
    partial_out = jnp.einsum("erf,efd->erd", hidden_low, w_down, preferred_element_type=jnp.float32)
    expert_low = lax.psum_scatter(
        partial_out.astype(jnp.bfloat16), "fsdp", scatter_dimension=1, tiled=True
    )
    returned = lax.all_to_all(
        expert_low.reshape(1, EXP_DEV, groups * capacity, MODEL_WIDTH),
        "expert",
        split_axis=2,
        concat_axis=0,
        tiled=True,
    ).reshape(experts_all * capacity, MODEL_WIDTH)
    expert_pair = returned[slot_ids].reshape(DEVICE_TOKENS, TOPK, MODEL_WIDTH)
    routed = jnp.sum(gate_share[:, :, None] * expert_pair, axis=1)
    block_out = (middle + routed).astype(jnp.bfloat16)
    upstream = cotangent.astype(jnp.float32)
    share_grad = jnp.sum(expert_pair * upstream[:, None, :], axis=-1)
    pair_grad = (
        (gate_share[:, :, None] * upstream[:, None, :])
        .astype(jnp.bfloat16)
        .reshape(pair_count, MODEL_WIDTH)
    )
    padded_grad = jnp.concatenate([pair_grad, jnp.zeros((1, MODEL_WIDTH), jnp.bfloat16)], axis=0)
    outgoing_grad = padded_grad[owner_pair].reshape(groups, EXP_DEV, capacity, MODEL_WIDTH)
    arrived_grad = lax.all_to_all(
        outgoing_grad, "expert", split_axis=0, concat_axis=2, tiled=True
    ).reshape(EXP_DEV, groups * capacity, MODEL_WIDTH)
    sigmoid_gate = jax.nn.sigmoid(gate_act)
    silu_gate = gate_act * sigmoid_gate
    group_grad = lax.all_gather(arrived_grad, "fsdp", axis=1, tiled=True)
    hidden_grad = jnp.einsum("erd,efd->erf", group_grad, w_down, preferred_element_type=jnp.float32)
    gate_grad_low = (
        hidden_grad * up_act * sigmoid_gate * (1.0 + gate_act * (1.0 - sigmoid_gate))
    ).astype(jnp.bfloat16)
    up_grad_low = (hidden_grad * silu_gate).astype(jnp.bfloat16)
    grad_w_gate = jnp.einsum(
        "erd,erf->edf", group_rows, gate_grad_low, preferred_element_type=jnp.float32
    )
    grad_w_up = jnp.einsum(
        "erd,erf->edf", group_rows, up_grad_low, preferred_element_type=jnp.float32
    )
    grad_w_down = jnp.einsum(
        "erf,erd->efd", hidden_low, group_grad, preferred_element_type=jnp.float32
    )
    partial_grad = jnp.einsum(
        "erf,edf->erd", gate_grad_low, w_gate, preferred_element_type=jnp.float32
    ) + jnp.einsum("erf,edf->erd", up_grad_low, w_up, preferred_element_type=jnp.float32)
    rows_grad = lax.psum_scatter(
        partial_grad.astype(jnp.bfloat16), "fsdp", scatter_dimension=1, tiled=True
    )
    back_rows = lax.all_to_all(
        rows_grad.reshape(1, EXP_DEV, groups * capacity, MODEL_WIDTH),
        "expert",
        split_axis=2,
        concat_axis=0,
        tiled=True,
    ).reshape(experts_all * capacity, MODEL_WIDTH)
    second_grad = jnp.sum(
        back_rows[slot_ids].reshape(DEVICE_TOKENS, TOPK, MODEL_WIDTH), axis=1, dtype=jnp.float32
    )
    mean_grad = jnp.sum(gate_share * share_grad, axis=1, keepdims=True)
    picked_grad = gate_share * (share_grad - mean_grad)
    logit_grad = jnp.sum(
        jnp.where(routes[:, :, None] == expert_ids[None, None, :], picked_grad[:, :, None], 0.0),
        axis=1,
    ).astype(jnp.bfloat16)
    router_grad = jnp.einsum("td,te->de", second, logit_grad, preferred_element_type=jnp.float32)
    second_grad = second_grad + jnp.einsum(
        "te,de->td", logit_grad, router_all, preferred_element_type=jnp.float32
    )
    ffn_gain_grad = jnp.sum(second_grad * ffn_unit, axis=0)
    middle_grad = upstream + norm_back(second_grad * ffn_gain_f, ffn_unit, ffn_inverse)
    branch_low = middle_grad.astype(jnp.bfloat16)
    out_grad = jnp.einsum("tc,td->cd", mixed_low, branch_low, preferred_element_type=jnp.float32)
    mixed_output_grad = jnp.einsum(
        "td,cd->tc", branch_low, out_all, preferred_element_type=jnp.float32
    ).astype(jnp.bfloat16)
    mixed_output_grad = mixed_output_grad.reshape(
        DEVICE_TOKENS, KEY_VALUE_HEADS, group_width, HEAD_WIDTH
    )
    probabilities = probabilities_of(query_head_groups, key_low, allowed, score_scale)
    value_gradient = jnp.einsum(
        "hgqk,qhgd->khd",
        probabilities.astype(jnp.bfloat16),
        mixed_output_grad,
        preferred_element_type=jnp.float32,
    )
    prob_grad = jnp.einsum(
        "qhgd,khd->hgqk", mixed_output_grad, value_low, preferred_element_type=jnp.float32
    )
    score_grad = (
        probabilities * (prob_grad - jnp.sum(probabilities * prob_grad, axis=-1, keepdims=True))
    ).astype(jnp.bfloat16)
    query_grad = (
        jnp.einsum(
            "hgqk,khd->qhgd", score_grad, key_low, preferred_element_type=jnp.float32
        ).reshape(DEVICE_TOKENS, QUERY_HEADS, HEAD_WIDTH)
        * score_scale
    )
    key_grad = (
        jnp.einsum(
            "hgqk,qhgd->khd", score_grad, query_head_groups, preferred_element_type=jnp.float32
        )
        * score_scale
    )
    query_turned = unrotate(query_grad, cosine, sine_table)
    query_gain_grad = jnp.sum(query_turned * query_unit, axis=(0, 1))
    query_raw_low = (
        norm_back(query_turned * query_gain_f, query_unit, query_inverse)
        .astype(jnp.bfloat16)
        .reshape(DEVICE_TOKENS, QUERY_HEADS * HEAD_WIDTH)
    )
    key_turned = unrotate(key_grad, cosine, sine_table)
    key_gain_grad = jnp.sum(key_turned * key_unit, axis=(0, 1))
    key_raw_low = (
        norm_back(key_turned * key_gain_f, key_unit, key_inverse)
        .astype(jnp.bfloat16)
        .reshape(DEVICE_TOKENS, KEY_VALUE_HEADS * HEAD_WIDTH)
    )
    value_gradient_lowered = value_gradient.astype(jnp.bfloat16).reshape(
        DEVICE_TOKENS, KEY_VALUE_HEADS * HEAD_WIDTH
    )
    query_wgrad = jnp.einsum(
        "td,tc->dc", normed_input, query_raw_low, preferred_element_type=jnp.float32
    )
    key_wgrad = jnp.einsum(
        "td,tc->dc", normed_input, key_raw_low, preferred_element_type=jnp.float32
    )
    value_wgrad = jnp.einsum(
        "td,tc->dc", normed_input, value_gradient_lowered, preferred_element_type=jnp.float32
    )
    normed_grad = (
        jnp.einsum("tc,dc->td", query_raw_low, query_all, preferred_element_type=jnp.float32)
        + jnp.einsum("tc,dc->td", key_raw_low, key_gathered, preferred_element_type=jnp.float32)
        + jnp.einsum(
            "tc,dc->td", value_gradient_lowered, value_all, preferred_element_type=jnp.float32
        )
    )
    attn_gain_grad = jnp.sum(normed_grad * attn_unit, axis=0)
    tokens_grad = middle_grad + norm_back(normed_grad * attn_gain_f, attn_unit, attn_inverse)
    owned = (
        lax.psum_scatter(
            attn_gain_grad.astype(jnp.bfloat16), "fsdp", scatter_dimension=0, tiled=True
        ).astype(jnp.float32),
        lax.psum_scatter(
            query_wgrad.astype(jnp.bfloat16), "fsdp", scatter_dimension=0, tiled=True
        ).astype(jnp.float32),
        lax.psum_scatter(
            key_wgrad.astype(jnp.bfloat16), "fsdp", scatter_dimension=0, tiled=True
        ).astype(jnp.float32),
        lax.psum_scatter(
            value_wgrad.astype(jnp.bfloat16), "fsdp", scatter_dimension=0, tiled=True
        ).astype(jnp.float32),
        lax.psum_scatter(
            out_grad.astype(jnp.bfloat16), "fsdp", scatter_dimension=0, tiled=True
        ).astype(jnp.float32),
        lax.psum_scatter(
            query_gain_grad.astype(jnp.bfloat16), "fsdp", scatter_dimension=0, tiled=True
        ).astype(jnp.float32),
        lax.psum_scatter(
            key_gain_grad.astype(jnp.bfloat16), "fsdp", scatter_dimension=0, tiled=True
        ).astype(jnp.float32),
        lax.psum_scatter(
            ffn_gain_grad.astype(jnp.bfloat16), "fsdp", scatter_dimension=0, tiled=True
        ).astype(jnp.float32),
        lax.psum_scatter(
            router_grad.astype(jnp.bfloat16), "fsdp", scatter_dimension=0, tiled=True
        ).astype(jnp.float32),
    )
    totals = (
        lax.psum(owned[0].astype(jnp.bfloat16), "expert").astype(jnp.float32),
        lax.psum(owned[1].astype(jnp.bfloat16), "expert").astype(jnp.float32),
        lax.psum(owned[2].astype(jnp.bfloat16), "expert").astype(jnp.float32),
        lax.psum(owned[3].astype(jnp.bfloat16), "expert").astype(jnp.float32),
        lax.psum(owned[4].astype(jnp.bfloat16), "expert").astype(jnp.float32),
        lax.psum(owned[5].astype(jnp.bfloat16), "expert").astype(jnp.float32),
        lax.psum(owned[6].astype(jnp.bfloat16), "expert").astype(jnp.float32),
        lax.psum(owned[7].astype(jnp.bfloat16), "expert").astype(jnp.float32),
        lax.psum(owned[8].astype(jnp.bfloat16), "expert").astype(jnp.float32),
    )
    return (
        block_out,
        tokens_grad,
        totals[0],
        totals[1],
        totals[2],
        totals[3],
        totals[4],
        totals[5],
        totals[6],
        totals[7],
        totals[8],
        grad_w_gate,
        grad_w_up,
        grad_w_down,
    )


def solution(mesh):
    return jax.shard_map(
        per_device,
        mesh=mesh,
        in_specs=(
            P(("expert", "fsdp"), None),
            P(("expert", "fsdp"), None),
            P(("expert", "fsdp"), None),
            P("fsdp"),
            P("fsdp", None),
            P("fsdp", None),
            P("fsdp", None),
            P("fsdp", None),
            P("fsdp"),
            P("fsdp"),
            P("fsdp"),
            P("fsdp", None),
            P("expert", None, "fsdp"),
            P("expert", None, "fsdp"),
            P("expert", "fsdp", None),
            P(("expert", "fsdp"), None),
        ),
        out_specs=(
            P(("expert", "fsdp"), None),
            P(("expert", "fsdp"), None),
            P("fsdp"),
            P("fsdp", None),
            P("fsdp", None),
            P("fsdp", None),
            P("fsdp", None),
            P("fsdp"),
            P("fsdp"),
            P("fsdp"),
            P("fsdp", None),
            P("expert", None, "fsdp"),
            P("expert", None, "fsdp"),
            P("expert", "fsdp", None),
        ),
        check_vma=False,
    )
```

profile of v0, /device:TPU:0, one launch (start us, length us, event | category | flops | bytes accessed | tf_op | source)
XLA Modules:
  0.0 3459.8 jit_solution(5678044655276611421)
XLA Ops:
  12.2 13.6 all-reduce.11
  25.9 12.1 all-gather.1
  38.0 12.1 all-gather
  65.0 39.9 %all-gather.11.cloned.1.call-done = bf16[2048,512]{1,0:T(8,128)(2,1)} async-done(((bf16[512,512]{1,0:T(8,128)(2,1)}), bf16[2048,512]{1,0:T(8,128)(2,1)}) %all-gather.11.cloned.1.call-update) | async-done | bytes 2097168 | tf_op jit(solution)/shard_map/all_gather | solution.py:104
  107.8 284.2 %all-gather.13.cloned.1.call-done = bf16[2048,4096]{1,0:T(8,128)(2,1)} async-done(((bf16[512,4096]{1,0:T(8,128)(2,1)}), bf16[2048,4096]{1,0:T(8,128)(2,1)}) %all-gather.13.cloned.1.call-update) | async-done | bytes 16777232 | tf_op jit(solution)/shard_map/all_gather | solution.py:103
  392.0 9.5 fusion.65
  414.9 263.5 %all-gather.15.cloned.1.call-done = bf16[4096,2048]{1,0:T(8,128)(2,1)} async-done(((bf16[1024,2048]{1,0:T(8,128)(2,1)}), bf16[4096,2048]{1,0:T(8,128)(2,1)}) %all-gather.15.cloned.1.call-update) | async-done | bytes 16777232 | tf_op jit(solution)/shard_map/all_gather | solution.py:106
  678.4 8.2 multiply_reduce_fusion.5
  687.8 7.0 gather_fusion
  694.8 75.2 %all_to_all.60 = bf16[8,2,96,2048]{3,2,1,0:T(8,128)(2,1)S(1)} all-to-all(bf16[8,2,96,2048]{3,2,1,0:T(8,128)(2,1)} %bitcast.217), channel_id=1, replica_groups=mesh['expert'=8,'fsdp'=4] {'expert'}, dimensions={0} | all-to-all | bytes 12582912 | tf_op jit(solution)/shard_map/all_to_all | solution.py:178
  774.8 13.6 all_gather.41
  789.2 7.0 gather_fusion.4
  799.9 15.4 gather_fusion.2
  815.3 75.2 %all_to_all.61 = bf16[8,2,96,2048]{3,2,1,0:T(8,128)(2,1)S(1)} all-to-all(bf16[8,2,96,2048]{3,2,1,0:T(8,128)(2,1)} %bitcast.218), channel_id=1, replica_groups=mesh['expert'=8,'fsdp'=4] {'expert'}, dimensions={0} | all-to-all | bytes 12582912 | tf_op jit(solution)/shard_map/all_to_all | solution.py:208
  893.9 300.1 %all-gather.17.cloned.1.call-done = bf16[2,3072,2048]{2,1,0:T(8,128)(2,1)} async-done(((bf16[2,768,2048]{2,1,0:T(8,128)(2,1)}), bf16[2,3072,2048]{2,1,0:T(8,128)(2,1)}) %all-gather.17.cloned.1.call-update) | async-done | bytes 25165840 | tf_op jit(solution)/shard_map/all_gather | solution.py:181
  1194.1 15.7 fusion.76
  1209.8 16.4 fusion.75
  1226.2 392.3 %all-gather.19.cloned.1.call-done = bf16[2,3072,2048]{2,1,0:T(8,128)(2,1)} async-done(((bf16[2,768,2048]{2,1,0:T(8,128)(2,1)}), bf16[2,3072,2048]{2,1,0:T(8,128)(2,1)}) %all-gather.19.cloned.1.call-update) | async-done | bytes 25165840 | tf_op jit(solution)/shard_map/all_gather | solution.py:213
  1618.5 18.2 multiply_convert_fusion
  1636.7 13.7 convolution_convert_fusion
  1651.7 21.2 fusion.77
  1673.0 26.5 add_convert_fusion
  1699.5 363.6 %reduce-scatter.8.cloned.1.call-done = bf16[2,768,2048]{2,1,0:T(8,128)(2,1)} async-done(((bf16[2,3072,2048]{2,1,0:T(8,128)(2,1)}), bf16[2,768,2048]{2,1,0:T(8,128)(2,1)}) %reduce-scatter.8.cloned.1.call-update) | async-done | bytes 6291472 | tf_op jit(solution)/shard_map/reduce_scatter | solution.py:186
  2063.1 12.6 copy.271
  2080.5 401.3 %reduce-scatter.10.cloned.1.call-done = bf16[2,768,2048]{2,1,0:T(8,128)(2,1)} async-done(((bf16[2,3072,2048]{2,1,0:T(8,128)(2,1)}), bf16[2,768,2048]{2,1,0:T(8,128)(2,1)}) %reduce-scatter.10.cloned.1.call-update) | async-done | bytes 6291472 | tf_op jit(solution)/shard_map/reduce_scatter | solution.py:231
  2481.8 12.6 copy.275
  2499.7 8.4 copy.272
  2508.1 12.5 gather_fusion.1
  2520.6 4.9 fusion.2
  2525.6 45.2 %all-to-all-done.3 = bf16[1,2,768,2048]{3,1,0,2:T(2,128)(2,1)} async-done(((bf16[1,2,768,2048]{3,1,0,2:T(2,128)(2,1)}), bf16[1,2,768,2048]{3,1,0,2:T(2,128)(2,1)}, u32[]{:S(2)}, u32[]{:S(2)}) %all-to-all-start.3) | async-done | bytes 6291488 | tf_op jit(solution)/shard_map/all_to_all | solution.py:234
  2570.8 8.4 copy.276
  2579.2 12.6 gather_fusion.3
  2591.8 5.1 convert_reduce_fusion
  2599.2 11.4 fusion.19
  2624.2 8.2 convolution_convert_fusion.1
  2666.2 6.5 fusion.7
  2672.7 8.3 convolution_convert_fusion.2
  2683.3 12.9 fusion.80
  2696.2 11.5 reduce-scatter.16.cloned.1.call-done
  2707.7 282.0 %reduce-scatter.18.cloned.1.call-done = bf16[1024,2048]{1,0:T(8,128)(2,1)} async-done(((bf16[4096,2048]{1,0:T(8,128)(2,1)}), bf16[1024,2048]{1,0:T(8,128)(2,1)}) %reduce-scatter.18.cloned.1.call-update) | async-done | bytes 4194320 | tf_op jit(solution)/shard_map/reduce_scatter | solution.py:337
  2989.7 283.4 %reduce-scatter.12.cloned.1.call-done = bf16[512,4096]{1,0:T(8,128)(2,1)} async-done(((bf16[2048,4096]{1,0:T(8,128)(2,1)}), bf16[512,4096]{1,0:T(8,128)(2,1)}) %reduce-scatter.12.cloned.1.call-update) | async-done | bytes 4194320 | tf_op jit(solution)/shard_map/reduce_scatter | solution.py:328
  3273.1 12.8 fusion.82
  3285.9 12.5 fusion.81
  3298.4 12.9 fusion.79
  3315.3 10.9 all-reduce.10
  3327.9 23.8 all-reduce.8
  3354.5 83.1 %all-reduce.14.cloned.1.call-done = (bf16[512,4096]{1,0:T(8,128)(2,1)}, bf16[512,512]{1,0:T(8,128)(2,1)}, bf16[512,512]{1,0:T(8,128)(2,1)}, bf16[1024,2048]{1,0:T(8,128)(2,1)}) async-done(((bf16[512,4096]{1,0:T(8,128)(2,1)}, bf16[512,512]{1,0:T(8,128)(2,1)}, bf16[512,512]{1,0:T(8,128)(2,1)}, bf16[1024,2048]{1,0:T(8,128)(2,1)}), (bf16[512,4096]{1,0:T(8,128)(2,1)}, bf16[512,512]{1,0:T(8,128)(2,1)}, ...) | async-done | bytes 9437200 | tf_op jit(solution)/shard_map/psum | solution.py:355
  3441.8 6.8 convert_element_type.238
  (324 shorter events, 127.4 us)
Async XLA Ops:
  7.2 1611.3 %copy-start = (bf16[2,192,2048]{2,1,0:T(8,128)(2,1)S(1)}, bf16[2,192,2048]{2,1,0:T(8,128)(2,1)}, u32[]{:S(2)}) copy-start(bf16[2,192,2048]{2,1,0:T(8,128)(2,1)} %param.30) | copy-start | bytes 4718596
  7.2 55.6 %all-gather.9.cloned.1.call-start = ((), (), s32[]{:S(2)}) async-start(), calls=%async_computation.11 | async-start | bytes 2621440 | tf_op jit(solution)/shard_map/all_gather | solution.py:105
  7.9 96.9 %all-gather.11.cloned.1.call-start = ((), (), s32[]{:S(2)}) async-start(), calls=%async_computation.12 | async-start | bytes 2621440 | tf_op jit(solution)/shard_map/all_gather | solution.py:104
  8.7 383.3 %all-gather.13.cloned.1.call-start = ((), (), s32[]{:S(2)}) async-start(), calls=%async_computation.13 | async-start | bytes 20971520 | tf_op jit(solution)/shard_map/all_gather | solution.py:103
  9.5 16.4 copy-start.72
  9.5 16.4 copy-start.73
  9.5 40.9 %copy-start.76 = (s32[1,4]{1,0:T(1,128)S(1)}, s32[1,4]{1,0:T(1,128)}, u32[]{:S(2)}) copy-start(s32[1,4]{1,0:T(1,128)} %param.17) | copy-start | bytes 52
  9.5 52.4 %copy-start.3 = (bf16[128,2048]{1,0:T(8,128)(2,1)S(1)}, bf16[128,2048]{1,0:T(8,128)(2,1)}, u32[]{:S(2)}) copy-start(bf16[128,2048]{1,0:T(8,128)(2,1)} %param.16) | copy-start | bytes 1572868
  9.5 668.9 %all-gather.15.cloned.1.call-start = ((), (), s32[]{:S(2)}) async-start(), calls=%async_computation.14 | async-start | bytes 20971520 | tf_op jit(solution)/shard_map/all_gather | solution.py:106
  10.1 1184.0 %all-gather.17.cloned.1.call-start = ((), (), s32[]{:S(2)}) async-start(), calls=%async_computation.15 | async-start | bytes 31457280 | tf_op jit(solution)/shard_map/all_gather | solution.py:181
  25.8 81.8 %copy-start.65 = (f32[128]{0:T(128)}, f32[128]{0:T(128)S(1)}, u32[]{:S(2)}) copy-start(f32[128]{0:T(128)S(1)} %convert_element_type.203) | copy-start | bytes 1540
  25.9 382.1 %copy-start.67 = (f32[128]{0:T(128)}, f32[128]{0:T(128)S(1)}, u32[]{:S(2)}) copy-start(f32[128]{0:T(128)S(1)} %convert_element_type.206) | copy-start | bytes 1540
  38.0 648.6 %copy-start.50 = (f32[4,1,512]{2,1,0:T(1,128)}, f32[4,1,512]{2,1,0:T(1,128)S(1)}, u32[]{:S(2)}) copy-start(f32[4,1,512]{2,1,0:T(1,128)S(1)} %convert_element_type.256) | copy-start | bytes 24580
  50.2 341.8 %copy-start.31 = (f32[4,1,512]{2,1,0:T(1,128)}, f32[4,1,512]{2,1,0:T(1,128)S(1)}, u32[]{:S(2)}) copy-start(f32[4,1,512]{2,1,0:T(1,128)S(1)} %convert_element_type.255) | copy-start | bytes 24580
  55.6 9.4 copy-start.63
  62.1 329.9 %copy-start.58 = (f32[128]{0:T(128)}, f32[128]{0:T(128)S(1)}, u32[]{:S(2)}) copy-start(f32[128]{0:T(128)S(1)} %add_rsqrt_fusion.3) | copy-start | bytes 1540
  65.0 348.4 %copy-start.40 = (bf16[128,4,128]{2,1,0:T(4,128)(2,1)}, bf16[128,4,128]{2,1,0:T(4,128)(2,1)S(1)}, u32[]{:S(2)}) copy-start(bf16[128,4,128]{2,1,0:T(4,128)(2,1)S(1)} %reshape.377) | copy-start | bytes 393220
  107.2 294.3 %copy-start.22 = (f32[128,4,128]{0,2,1:T(8,128)}, f32[128,4,128]{0,2,1:T(8,128)S(1)}, u32[]{:S(2)}) copy-start(f32[128,4,128]{0,2,1:T(8,128)S(1)} %copy.255) | copy-start | bytes 786436
  107.5 294.0 %copy-start.56 = (f32[128,4]{0,1:T(4,128)}, f32[128,4]{0,1:T(4,128)S(1)}, u32[]{:S(2)}) copy-start(f32[128,4]{0,1:T(4,128)S(1)} %add_rsqrt_fusion.1) | copy-start | bytes 6148
  107.7 300.8 %copy-start.42 = (bf16[128,4,128,1]{0,2,3,1:T(8,128)(2,1)}, bf16[128,4,128,1]{0,2,3,1:T(8,128)(2,1)S(1)}, u32[]{:S(2)}) copy-start(bf16[128,4,128,1]{0,2,3,1:T(8,128)(2,1)S(1)} %fusion.37) | copy-start | bytes 393220
  414.8 271.8 %copy-start.9 = (bf16[4,128,8,128]{3,1,2,0:T(8,128)(2,1)}, bf16[4,128,8,128]{3,1,2,0:T(8,128)(2,1)S(1)}, u32[]{:S(2)}) copy-start(bf16[4,128,8,128]{3,1,2,0:T(8,128)(2,1)S(1)} %convolution_convert_fusion.7) | copy-start | bytes 3145732
  686.6 8.1 copy-start.69
  687.7 100.6 %copy-start.18 = (bf16[128,2048]{1,0:T(8,128)(2,1)}, bf16[128,2048]{1,0:T(8,128)(2,1)S(1)}, u32[]{:S(2)}) copy-start(bf16[128,2048]{1,0:T(8,128)(2,1)S(1)} %multiply_convert_fusion.3) | copy-start | bytes 1572868
  773.3 845.2 %all-gather.19.cloned.1.call-start = ((), (), s32[]{:S(2)}) async-start(), calls=%async_computation.17 | async-start | bytes 31457280 | tf_op jit(solution)/shard_map/all_gather | solution.py:213
  774.7 21.9 copy-start.15
  893.8 300.2 %copy-start.29 = (bf16[2,2048,192]{1,2,0:T(8,128)(2,1)S(1)}, bf16[2,2048,192]{1,2,0:T(8,128)(2,1)}, u32[]{:S(2)}) copy-start(bf16[2,2048,192]{1,2,0:T(8,128)(2,1)} %param.29) | copy-start | bytes 4718596
  893.9 1169.2 %reduce-scatter.8.cloned.1.call-start = ((), (), s32[]{:S(2)}) async-start(), calls=%async_computation.16 | async-start | bytes 31457280 | tf_op jit(solution)/shard_map/reduce_scatter | solution.py:186
  1650.4 831.4 %reduce-scatter.10.cloned.1.call-start = ((), (), s32[]{:S(2)}) async-start(), calls=%async_computation.18 | async-start | bytes 31457280 | tf_op jit(solution)/shard_map/reduce_scatter | solution.py:231
  2075.7 418.7 %all-to-all-start.1 = ((bf16[1,2,768,2048]{3,1,0,2:T(2,128)(2,1)}), bf16[1,2,768,2048]{3,1,0,2:T(2,128)(2,1)}, u32[]{:S(2)}, u32[]{:S(2)}) async-start(bf16[1,2,768,2048]{3,1,0,2:T(2,128)(2,1)} %copy.271), calls=%async_computation.2 | async-start | bytes 12582912 | tf_op jit(solution)/shard_map/all_to_all | solution.py:189
  2494.4 5.2 copy-start.64
  2494.4 76.4 %all-to-all-start.3 = ((bf16[1,2,768,2048]{3,1,0,2:T(2,128)(2,1)}), bf16[1,2,768,2048]{3,1,0,2:T(2,128)(2,1)}, u32[]{:S(2)}, u32[]{:S(2)}) async-start(bf16[1,2,768,2048]{3,1,0,2:T(2,128)(2,1)} %copy.275), calls=%async_computation.5 | async-start | bytes 12582912 | tf_op jit(solution)/shard_map/all_to_all | solution.py:234
  2499.2 197.0 %reduce-scatter.14.cloned.1.call-start = ((), (), s32[]{:S(2)}) async-start(), calls=%async_computation.20 | async-start | bytes 2621440 | tf_op jit(solution)/shard_map/reduce_scatter | solution.py:331
  2508.1 12.5 copy-start.16
  2508.1 12.5 copy-start.36
  2520.6 5.0 copy-start.45
  2591.8 5.2 copy-start.8
  2591.8 5.2 copy-start.38
  2591.8 5.2 copy-start.51
  2591.8 5.2 copy-start.70
  2599.2 11.7 copy-start.41
  2599.2 11.7 copy-start.53
  2618.2 89.5 %reduce-scatter.16.cloned.1.call-start = ((), (), s32[]{:S(2)}) async-start(), calls=%async_computation.21 | async-start | bytes 2621440 | tf_op jit(solution)/shard_map/reduce_scatter | solution.py:334
  2624.1 365.6 %reduce-scatter.18.cloned.1.call-start = ((), (), s32[]{:S(2)}) async-start(), calls=%async_computation.22 | async-start | bytes 20971520 | tf_op jit(solution)/shard_map/reduce_scatter | solution.py:337
  2632.4 640.7 %reduce-scatter.12.cloned.1.call-start = ((), (), s32[]{:S(2)}) async-start(), calls=%async_computation.19 | async-start | bytes 20971520 | tf_op jit(solution)/shard_map/reduce_scatter | solution.py:328
  2681.0 646.8 %reduce-scatter.20.cloned.1.call-start = ((), (), s32[]{:S(2)}) async-start(), calls=%async_computation.23 | async-start | bytes 81920 | tf_op jit(solution)/shard_map/reduce_scatter | solution.py:349
  2683.3 754.3 %all-reduce.14.cloned.1.call-start = ((), (), s32[]{:S(2)}) async-start(), calls=%async_computation.24 | async-start | bytes 18874368 | tf_op jit(solution)/shard_map/psum | solution.py:355
  3273.1 12.8 copy-start.5
  3441.8 6.8 copy-start.24
  (45 other events, 85.9 us)
Sparse Core Ops, SparseCore 0:
  9.6 48.8 all-gather.8
  60.1 44.7 all-gather.10
  106.4 285.4 all-gather.12
  393.4 284.9 all-gather.14
  773.4 420.5 all-gather.16
  1196.1 422.3 all-gather.18
  1650.5 412.5 reduce-scatter.7
  2065.6 416.1 reduce-scatter.9
  2618.3 43.8 reduce-scatter.13
  2664.5 43.1 reduce-scatter.15
  2710.0 279.5 reduce-scatter.17
  2992.0 281.0 reduce-scatter.11
  3275.9 19.7 reduce-scatter.19
  3300.0 137.4 all-reduce.13
where the time goes:
time: 3460 us
  waiting for transfers between devices  2750 us (79%)
  blocking collectives  237 us (7%)
  matrix products  233 us (7%)
  local copies, waits for them, and re-layouts  144 us (4%)
  other arithmetic  65.5 us (2%)
    reduce_scatter x1, waiting for transfers between devices, per_device(): lax.psum_scatter(partial_grad.astype(jnp.bfloat16), 'fsdp', scatter_dimen...  401 us
    all_gather x1, waiting for transfers between devices, per_device(): group_grad = lax.all_gather(arrived_grad, 'fsdp', axis=1, tiled=True)  392 us
    reduce_scatter x1, waiting for transfers between devices, per_device(): lax.psum_scatter(partial_out.astype(jnp.bfloat16), 'fsdp', scatter_dimens...  364 us
    all_gather x1, waiting for transfers between devices, per_device(): group_rows = lax.all_gather(arrived, 'fsdp', axis=1, tiled=True)  300 us
    all_gather x1, waiting for transfers between devices, per_device(): lax.all_gather(w_query, 'fsdp', axis=0, tiled=True)  284 us
    reduce_scatter x1, waiting for transfers between devices, per_device(): lax.psum_scatter(query_wgrad.astype(jnp.bfloat16), 'fsdp', scatter_dimens...  283 us
    reduce_scatter x1, waiting for transfers between devices, per_device(): lax.psum_scatter(out_grad.astype(jnp.bfloat16), 'fsdp', scatter_dimension...  282 us
    all_gather x1, waiting for transfers between devices, per_device(): lax.all_gather(w_out, 'fsdp', axis=0, tiled=True)  264 us
  transfers between devices with their start and end apart: 16, of which 12 were waited for; matrix products, arithmetic and copies ran while one was open for 9% of the time, Pallas kernels for 0%

commit v1 on v0

v1 whole, which is shorter than its diff:
```python
import jax
import jax.numpy as jnp
import ml_dtypes
import numpy as np
from jax import lax
from jax.experimental import pallas as pl
from jax.experimental.pallas import tpu as pltpu
from jax.sharding import PartitionSpec as P

MODEL_WIDTH = 2048
QUERY_HEADS = 32
KEY_VALUE_HEADS = 4
HEAD_WIDTH = 128
TOPK = 8
DEVICE_TOKENS = 128
SEQ_SLOTS = 4

epsilon = 1e-06
rope_base = 1000000.0
masked_score = -1e30
BF = jnp.bfloat16
F32 = jnp.float32


def layout(lengths_row, tok_count, slot_count):
    seq_ends = jnp.cumsum(lengths_row)
    starts = seq_ends - lengths_row
    places = jnp.arange(tok_count, dtype=jnp.int32)
    segment = jnp.sum((places[:, None] >= seq_ends[None, :]).astype(jnp.int32), axis=1)
    member = segment[:, None] == jnp.arange(slot_count, dtype=jnp.int32)[None, :]
    start_of = jnp.sum(jnp.where(member, starts[None, :], 0), axis=1)
    return (places - start_of, segment)


def rope_tables(places, head_size):
    frequency = rope_base ** (-jnp.arange(0, head_size, 2, dtype=jnp.float32) / head_size)
    angles = places.astype(jnp.float32)[..., None] * frequency
    angles = jnp.concatenate([angles, angles], axis=-1)
    return (jnp.cos(angles), jnp.sin(angles))


def rotate(values, cosine, sine_table):
    half_width = values.shape[-1] // 2
    turned = jnp.concatenate([-values[..., half_width:], values[..., :half_width]], axis=-1)
    return values * cosine + turned * sine_table


def unrotate(gradient, cosine, sine_table):
    scaled = gradient * sine_table
    half_width = gradient.shape[-1] // 2
    return gradient * cosine + jnp.concatenate(
        [scaled[..., half_width:], -scaled[..., :half_width]], axis=-1
    )


def norm_back(gradient, unit_value, inverse):
    return inverse * (
        gradient - unit_value * jnp.mean(gradient * unit_value, axis=-1, keepdims=True)
    )


def dot(a, b, dims):
    return lax.dot_general(a, b, (dims, ((), ())), preferred_element_type=F32)


NN = ((1,), (0,))
NT = ((1,), (1,))
TN = ((0,), (0,))
VMEM_BYTES = 63 * 1024 * 1024

MESH = pl.DeviceIdType.MESH
EXTRA = 128
DIAG, XCOL, YCOL, OWN = 0, 1, 2, 3


def remote(src, dst, send, recv, device):
    return pltpu.make_async_remote_copy(
        src_ref=src,
        dst_ref=dst,
        send_sem=send,
        recv_sem=recv,
        device_id=device,
        device_id_type=MESH,
    )


class Place:
    def __init__(self):
        e = lax.axis_index("expert")
        z = lax.axis_index("fsdp")
        self.e, self.z = e, z
        self.core = lax.rem(e, 2)
        self.x = lax.rem(lax.div(e, 2), 2)
        self.y = lax.div(e, 4)
        self.x_near = (e + 2 - 4 * self.x, z)
        self.y_near = (e + 4 - 8 * self.y, z)
        self.sibling = (e + 1 - 2 * self.core, z)
        self.diagonal = (1 - self.y) * 4 + (1 - self.x) * 2 + self.core
        self.partner = z + 1 - 2 * lax.rem(z, 2)
        self.half = lax.div(z, 2)

    def plane(self, k):
        far = jnp.where(self.half == 0, k, 3 - k)
        return jnp.where(k == 0, self.z, jnp.where(k == 1, self.partner, far))

    def turn_at(self, z_there):
        far = jnp.where(z_there < 2, self.z, 3 - self.z)
        return jnp.where(z_there == self.partner, 1, far)

    def column_base(self, q):
        x = self.x if q in (YCOL, OWN) else 1 - self.x
        y = self.y if q in (XCOL, OWN) else 1 - self.y
        return (y * 2 + x) * 2

    def own(self, q):
        return self.column_base(q) + self.core

    def everyone(self):
        return [self.x_near, self.y_near, self.sibling] + [(self.e, self.plane(k)) for k in (1, 2, 3)]


def when(condition):
    def run(body):
        if isinstance(condition, bool):
            if condition:
                body()
        else:
            pl.when(condition)(body)

    return run


def greet(devices):
    barrier = pltpu.get_barrier_semaphore()
    for device in devices:
        pl.semaphore_signal(barrier, inc=1, device_id=device, device_id_type=MESH)


def meet(devices, greeted=False):
    if not greeted:
        greet(devices)
    pl.semaphore_wait(pltpu.get_barrier_semaphore(), len(devices))


class Line:
    def __init__(self, at, block, sems):
        self.at, self.block = at, block
        self.send, self.recv = sems

    def up(self, b):
        block = self.block(b)
        return remote(
            block, block, self.send.at[0, b], self.recv.at[b], (self.at.e, self.at.z + 1)
        )

    def down(self, b):
        block = self.block(b)
        return remote(
            block, block, self.send.at[1, b], self.recv.at[b], (self.at.e, self.at.z - 1)
        )

    def begin(self):
        z = self.at.z

        @pl.when(z < 3)
        def _():
            self.up(z).start()

        @pl.when(z > 0)
        def _():
            self.down(z).start()

    def arrive(self, k):
        z = self.at.z
        b = self.at.plane(k)
        block = self.block(b)
        remote(block, block, self.send.at[0, b], self.recv.at[b], self.at.sibling).wait_recv()

        @pl.when((b < z) & (z < 3))
        def _():
            self.up(b).start()

        @pl.when((b > z) & (z > 0))
        def _():
            self.down(b).start()

    def end(self):
        z = self.at.z
        for b in range(4):

            @pl.when((b <= z) & (z < 3))
            def _():
                self.up(b).wait_send()

            @pl.when((b >= z) & (z > 0))
            def _():
                self.down(b).wait_send()

    @staticmethod
    def semaphores():
        return [pltpu.SemaphoreType.DMA((2, 4)), pltpu.SemaphoreType.DMA((4,))]


class LineSum:
    def __init__(self, at, part, came, sems):
        self.at, self.part, self.came = at, part, came
        self.send, self.recv = sems

    def arrival(self, slot):
        block = self.came.at[slot]
        return remote(block, block, self.send.at[0], self.recv.at[slot], self.at.sibling)

    def copy(self, t):
        z = self.at.z
        up = (t > z).astype(jnp.int32)
        there = z + 2 * up - 1
        slot = jnp.where((t == there) & (up == 0), 4, t)
        return remote(
            self.part.at[t], self.came.at[slot], self.send.at[t], self.recv.at[slot], (self.at.e, there)
        )

    def give(self, t):
        z = self.at.z

        @pl.when(((t > z) & (z > 0)) | ((t < z) & (z < 3)))
        def _():
            self.arrival(t).wait_recv()

            @pl.loop(0, self.part.shape[1] // 32)
            def _(i):
                here = pl.ds(pl.multiple_of(i * 32, 32), 32)
                self.part[t, here] = (
                    self.part[t, here].astype(F32) + self.came[t, here].astype(F32)
                ).astype(BF)

        self.copy(t).start()

    def give_far(self):
        half = self.at.half
        self.give(jnp.where(half == 0, 3, 0))
        self.give(jnp.where(half == 0, 2, 1))

    def give_near(self, early):
        z = self.at.z
        outer = (z == 0) | (z == 3)

        @pl.when(outer if early else jnp.logical_not(outer))
        def _():
            self.give(self.at.partner)

    def wait(self):
        z = self.at.z
        zero = jnp.zeros(self.came.shape[1:], BF)

        @pl.when(z > 0)
        def _():
            self.arrival(z).wait_recv()

        @pl.when(z == 0)
        def _():
            self.came[0] = zero

        @pl.when(z < 3)
        def _():
            self.arrival(4).wait_recv()

        @pl.when(z == 3)
        def _():
            self.came[4] = zero

    def total(self, here):
        return self.came[self.at.z, here].astype(F32) + self.came[4, here].astype(F32)

    def end(self):
        for t in range(4):

            @pl.when(t != self.at.z)
            def _():
                self.copy(t).wait_send()

    @staticmethod
    def semaphores():
        return [pltpu.SemaphoreType.DMA((4,)), pltpu.SemaphoreType.DMA((5,))]


class Gather:
    def __init__(self, at, block, sems, sibling=True):
        self.at, self.block, self.sibling = at, block, sibling
        (self.x_send, self.x_recv, self.y_send, self.y_recv) = sems[:4]
        self.half_send, self.half_recv = sems[4:6]
        if sibling:
            self.sib_send, self.sib_recv = sems[6:8]

    def to_x(self, k):
        block = self.block(k, OWN)
        return remote(block, block, self.x_send.at[k], self.x_recv.at[k], self.at.x_near)

    def to_y(self, k):
        block = self.block(k, OWN)
        return remote(block, block, self.y_send.at[k], self.y_recv.at[k], self.at.y_near)

    def on_y(self, k):
        block = self.block(k, XCOL, 0)
        sem = 2 * k
        return remote(block, block, self.half_send.at[sem], self.half_recv.at[sem], self.at.y_near)

    def on_x(self, k):
        block = self.block(k, YCOL, 1)
        sem = 2 * k + 1
        return remote(block, block, self.half_send.at[sem], self.half_recv.at[sem], self.at.x_near)

    def to_sib(self, k, q):
        block = self.block(k, q)
        sem = 4 * k + q
        return remote(block, block, self.sib_send.at[sem], self.sib_recv.at[sem], self.at.sibling)

    def share(self, k, q):
        if self.sibling:
            self.to_sib(k, q).start()

    def own(self, k):
        self.to_x(k).start()
        self.to_y(k).start()
        self.share(k, OWN)

    def cross(self, k, halves=True):
        self.to_x(k).wait_recv()
        if halves:
            self.on_y(k).start()
        self.share(k, XCOL)
        self.to_y(k).wait_recv()
        if halves:
            self.on_x(k).start()
        self.share(k, YCOL)

    def diag(self, k):
        self.on_y(k).wait_recv()
        self.on_x(k).wait_recv()
        self.share(k, DIAG)

    def ready(self, k, q):
        self.to_sib(k, q).wait_recv()

    def end(self, k, halves=True):
        self.to_x(k).wait_send()
        self.to_y(k).wait_send()
        if halves:
            self.on_x(k).wait_send()
            self.on_y(k).wait_send()
        for q in range(4) if self.sibling else ():
            self.to_sib(k, q).wait_send()

    @staticmethod
    def semaphores(sibling=True):
        dma = pltpu.SemaphoreType.DMA
        return [dma((4,))] * 4 + [dma((8,))] * 2 + [dma((16,))] * 2 * sibling


def expert_kernel(
    second_ref,
    cot_ref,
    gate_ref,
    up_ref,
    down_ref,
    sums_ref,
    gate_grad_ref,
    up_grad_ref,
    down_grad_ref,
    kept_ref,
    held,
    part,
    diag_a,
    diag_b,
    diag_z,
    x_whole,
    y_whole,
    z_part,
    pair_part,
    cot_tile,
    gate_up,
    down,
    acts,
    back,
    gate_tile,
    hidden_tile,
    kept_tile,
    grad_tile,
    widen,
    narrow,
    load_sem,
    gift_send,
    gift_recv,
    cot_sem,
    kept_sem,
    grad_sem,
    reload_sem,
    over_sem,
    red_send,
    red_recv,
    zr_send,
    zr_recv,
    pair_send,
    pair_recv,
    give_send,
    give_recv,
    give_ready,
    *sems,
):
    at = Place()
    rows = second_ref.shape[0]
    pair, quad = 2 * rows, 4 * rows
    total_rows, carried = held.shape
    model = cot_ref.shape[1]
    wide = down.shape[0]
    own_wide = wide // 2
    units = wide // 4
    half = rows // 2
    partner = (at.e, at.partner)
    experts_all = 16
    loads, gifts = [], []
    for i, (ref, held_weights, first) in enumerate(
        ((gate_ref, gate_up, 0), (up_ref, gate_up, wide), (down_ref, down, 0))
    ):
        here = pl.ds(pl.multiple_of(first + at.core * own_wide, own_wide), own_wide)
        loads.append(pltpu.make_async_copy(ref, held_weights.at[here], load_sem.at[i]))
        gifts.append(
            remote(ref, held_weights.at[here], gift_send.at[i], gift_recv.at[i], at.sibling)
        )
    for copy in loads:
        copy.start()

    def named(shape, unit_axis):
        unit = lax.broadcasted_iota(jnp.int32, shape, unit_axis)
        lane = lax.broadcasted_iota(jnp.int32, shape, 1 - unit_axis)
        expert = at.e // 2 * 4
        for i in (1, 2, 3):
            expert = expert + (unit >= i * units).astype(jnp.int32)
        return ((lane == expert) | (lane == expert + experts_all)).astype(F32).astype(BF)

    widen[...] = named((EXTRA, wide), 1)
    narrow[...] = named((wide, EXTRA), 0)
    meet(at.everyone())
    for copy in gifts:
        copy.start()

    def side_first(k, side):
        return (at.plane(k) * 4 + (at.y if side else 1 - at.y) * 2) * rows

    def side_rows(k, side):
        return pl.ds(pl.multiple_of(side_first(k, side), pair), pair)

    def block(k, q, i=None):
        first, count = (0, rows) if i is None else (i * half, half)
        first = (at.plane(k) * 4 + at.column_base(q) // 2) * rows + first
        return held.at[pl.ds(pl.multiple_of(first, half), count)]

    def line_block(b):
        first = (b * 4 + at.column_base(OWN) // 2) * rows
        return held.at[pl.ds(pl.multiple_of(first, rows), rows)]

    line = Line(at, line_block, sems[:2])
    gather = Gather(at, block, sems[2:], sibling=False)
    first_row = (at.z * 4 + at.column_base(OWN) // 2) * rows
    held[pl.ds(pl.multiple_of(first_row, rows), rows)] = second_ref[...]
    line.begin()
    gather.own(0)

    def over_z(k):
        there = block(k, DIAG)
        return remote(there, there, over_sem.at[0], over_sem.at[1], partner)

    def cot_copy(k, side):
        return pltpu.make_async_copy(cot_ref.at[side_rows(k, side)], cot_tile, cot_sem)

    def kept_copy(k, side):
        return pltpu.make_async_copy(kept_tile, kept_ref.at[:, side_rows(k, side)], kept_sem)

    def compute(r, k, side, following):
        here = side_rows(k, side)
        acts[...] = lax.dot_general(
            held[here, :model], gate_up[...], (NT, ((), ())), preferred_element_type=F32
        )
        cot_copy(k, side).wait()
        back[...] = lax.dot_general(
            cot_tile[...], down[...], (NT, ((), ())), preferred_element_type=F32
        )
        following()

        @when(not (isinstance(r, int) and r == 0 and side == 1))
        def _():
            kept_copy(k, side).wait()

        out_first = r * quad + side * pair
        for i in range(pair // rows):
            strip_rows = slice(i * rows, (i + 1) * rows)
            first = side_first(k, side) + i * rows
            share_rows = held[pl.ds(pl.multiple_of(first, rows), rows), model:]
            gate_act, up_act = acts[strip_rows, :wide], acts[strip_rows, wide:]
            raw_back = back[strip_rows]
            share = jnp.dot(share_rows, widen[...], preferred_element_type=F32)
            sigmoid = 1.0 / (1.0 + jnp.exp(-gate_act))
            silu = gate_act * sigmoid
            hidden = silu * up_act
            product = hidden * raw_back
            high = product.astype(BF)
            low = (product - high.astype(F32)).astype(BF)
            share_grad = jnp.dot(high, narrow[...], preferred_element_type=F32) + jnp.dot(
                low, narrow[...], preferred_element_type=F32
            )
            lane = lax.broadcasted_iota(jnp.int32, share_grad.shape, 1)
            rounded = share_grad.astype(BF).astype(F32)
            share_grad = jnp.where(lane < experts_all, rounded, share_grad - rounded)
            hidden_low = (share * hidden).astype(BF)
            hidden_grad = share * raw_back
            gate_grad = (
                hidden_grad * up_act * sigmoid * (1.0 + gate_act * (1.0 - sigmoid))
            ).astype(BF)
            up_grad = (hidden_grad * silu).astype(BF)
            gate_tile[strip_rows, :wide] = gate_grad
            gate_tile[strip_rows, wide:] = up_grad
            hidden_tile[strip_rows] = hidden_low
            kept_tile[:wide, strip_rows] = gate_grad.T
            kept_tile[wide : 2 * wide, strip_rows] = up_grad.T
            kept_tile[2 * wide :, strip_rows] = hidden_low.T
            out_rows = pl.ds(pl.multiple_of(out_first + i * rows, rows), rows)
            part[out_rows, 2 * model :] = share_grad.astype(BF)
        kept_copy(k, side).start()
        there = pl.ds(pl.multiple_of(out_first, pair), pair)
        step = 512
        for start in range(0, model, step):
            part[there, start : start + step] = jnp.dot(
                hidden_tile[...], down[:, start : start + step], preferred_element_type=F32
            ).astype(BF)
            part[there, model + start : model + start + step] = jnp.dot(
                gate_tile[...], gate_up[:, start : start + step], preferred_element_type=F32
            ).astype(BF)

    def part_row(r, q, first=0):
        x = at.x if q in (YCOL, OWN) else 1 - at.x
        return r * quad + (pair if q in (XCOL, OWN) else 0) + x * rows + first

    def part_rows(r, q, first, count):
        return pl.ds(pl.multiple_of(part_row(r, q, first), min(count, half)), count)

    def half_a(r):
        src = part.at[part_rows(r, DIAG, 0, half)]
        return remote(src, diag_a.at[r % 2], red_send.at[0, r], red_recv.at[0, r], at.y_near)

    def half_b(r):
        src = part.at[part_rows(r, DIAG, half, half)]
        return remote(src, diag_b.at[r % 2], red_send.at[1, r], red_recv.at[1, r], at.x_near)

    def x_copy(r):
        src = part.at[part_rows(r, XCOL, 0, rows)]
        return remote(src, x_whole.at[r % 2], red_send.at[2, r], red_recv.at[2, r], at.x_near)

    def y_copy(r):
        src = part.at[part_rows(r, YCOL, 0, rows)]
        return remote(src, y_whole.at[r % 2], red_send.at[3, r], red_recv.at[3, r], at.y_near)

    def diag_over():
        src = part.at[part_rows(0, DIAG, 0, rows)]
        return remote(src, diag_z, red_send.at[0, 0], red_recv.at[0, 0], partner)

    strip = 32

    def by_strips(count, body):
        @pl.loop(0, count // strip)
        def _(i):
            body(pl.multiple_of(i * strip, strip))

    def reduce_diag(r):
        @when(r == 3)
        def _():
            diag_over().wait_recv()

            def body(row):
                here = part_rows(r, DIAG, row, strip)
                part[here] = (
                    part[here].astype(F32) + diag_z[pl.ds(row, strip)].astype(F32)
                ).astype(BF)

            by_strips(rows, body)

        @when(r == 0)
        def _():
            diag_over().start()

        @when(r > 0)
        def _():
            half_a(r).start()
            half_b(r).start()

    def reduce_x(r):
        @when(r > 0)
        def _():
            half_a(r).wait_recv()

            def body(row):
                here = part_rows(r, XCOL, row, strip)
                part[here] = (
                    part[here].astype(F32) + diag_a[r % 2, pl.ds(row, strip)].astype(F32)
                ).astype(BF)

            by_strips(half, body)

        x_copy(r).start()

    def reduce_y(r):
        @when(r > 0)
        def _():
            half_b(r).wait_recv()

            def body(row):
                here = part_rows(r, YCOL, half + row, strip)
                part[here] = (
                    part[here].astype(F32) + diag_b[r % 2, pl.ds(row, strip)].astype(F32)
                ).astype(BF)

            by_strips(half, body)

        y_copy(r).start()

    inner = (at.z == 1) | (at.z == 2)

    def near_copy():
        src = part.at[part_rows(0, OWN, 0, rows)]
        return remote(src, z_part.at[0], zr_send.at[0], zr_recv.at[0], partner)

    def pair_copy(r):
        block = pair_part.at[r - 1]
        return remote(block, block, pair_send.at[r - 1], pair_recv.at[r - 1], partner)

    def far_copy(r):
        there = at.plane(r + 1)
        return remote(
            pair_part.at[r - 1], z_part.at[1], zr_send.at[r], zr_recv.at[1], (at.e, there)
        )

    def pass_on(r):
        @pl.when(inner)
        def _():
            pair_copy(r).wait_recv()

            def body(row):
                here = pl.ds(row, strip)
                pair_part[r - 1, here] = (
                    pair_part[r - 1, here].astype(F32)
                    + part[part_rows(r, OWN, row, strip)].astype(F32)
                ).astype(BF)

            by_strips(rows, body)
            far_copy(r).start()

    def reduce_own(r):
        x_copy(r).wait_recv()
        y_copy(r).wait_recv()

        def total(row):
            here = pl.ds(row, strip)
            return (
                part[part_rows(r, OWN, row, strip)].astype(F32)
                + x_whole[r % 2, here].astype(F32)
                + y_whole[r % 2, here].astype(F32)
            )

        @when(r == 3)
        def _():
            near_copy().wait_recv()
            block = z_part.at[1]
            remote(block, block, zr_send.at[0], zr_recv.at[1], at.sibling).wait_recv()

            def body(row):
                here = pl.ds(row, strip)
                sums_ref[here] = total(row) + (
                    z_part[0, here].astype(F32) + z_part[1, here].astype(F32)
                )

            by_strips(rows, body)

        def keep(row):
            part[part_rows(r, OWN, row, strip)] = total(row).astype(BF)

        def lay_out(row):
            pair_part[r - 1, pl.ds(row, strip)] = total(row).astype(BF)

        @when(r == 0)
        def _():
            by_strips(rows, keep)
            near_copy().start()

        @when(between(r, 1, 2))
        def _():
            @pl.when(inner)
            def _():
                by_strips(rows, keep)

            @pl.when(jnp.logical_not(inner))
            def _():
                by_strips(rows, lay_out)
                pair_copy(r).start()

    def far_rows(k):
        line.arrive(k)
        gather.own(k)

    cot_copy(1, 1).start()
    line.arrive(1)
    gather.own(1)

    @pl.when(inner)
    def _():
        far_rows(2)

    gather.cross(0)
    gather.cross(1, halves=False)

    @pl.when(inner)
    def _():
        far_rows(3)

    for copy in loads + gifts:
        copy.wait()
    compute(0, 1, 1, lambda: cot_copy(1, 0).start())
    reduce_x(0)
    gather.diag(0)
    over_z(0).start()

    @pl.when(jnp.logical_not(inner))
    def _():
        far_rows(2)

    over_z(1).wait_recv()
    compute(0, 1, 0, lambda: cot_copy(2, 0).start())
    reduce_y(0)
    reduce_diag(0)

    @pl.when(jnp.logical_not(inner))
    def _():
        far_rows(3)

    gather.cross(2)
    gather.diag(2)
    compute(1, 2, 0, lambda: cot_copy(2, 1).start())
    reduce_diag(1)
    gather.cross(3)

    @pl.loop(1, 3)
    def _(r):
        k, later = r + 1, lax.rem(r + 2, 4)
        compute(r, k, 1, lambda: cot_copy(later, 0).start())
        reduce_own(r - 1)

        @pl.when(r == 1)
        def _():
            gather.diag(3)

        compute(r + 1, later, 0, lambda: cot_copy(later, 1).start())
        reduce_x(r)
        reduce_y(r)

        @pl.when(r == 2)
        def _():
            pass_on(1)

        reduce_diag(r + 1)

    compute(3, 0, 1, lambda: None)

    line.end()
    over_z(0).wait_send()
    diag_over().wait_send()
    near_copy().wait_send()
    x_copy(0).wait_send()
    y_copy(0).wait_send()
    for copy in (half_a(1), half_b(1), x_copy(1), y_copy(1)):
        copy.wait_send()
    pl.semaphore_signal(give_ready, inc=1, device_id=at.sibling, device_id_type=MESH)
    for k in range(4):
        gather.end(k, halves=k != 1)
    kept_copy(0, 1).wait()
    turned = [
        pltpu.make_async_copy(kept_ref.at[pl.ds(0, 2 * wide)], gate_up, load_sem.at[0]),
        pltpu.make_async_copy(kept_ref.at[pl.ds(2 * wide, wide)], down, load_sem.at[1]),
    ]
    for copy in turned:
        copy.start()
    step = 256
    chunks = model // step
    mine, theirs = at.core * own_wide, (1 - at.core) * own_wide

    def lanes_of(n):
        return pl.ds(pl.multiple_of(n * step, step), step)

    def turned_rows(first):
        return pl.ds(pl.multiple_of(first, own_wide), own_wide)

    def given(i, first, size):
        return part.at[pl.ds(0, own_wide), pl.ds(pl.multiple_of(i * model + first, step), size)]

    def taken(i, first, size):
        return part.at[pl.ds(quad, own_wide), pl.ds(pl.multiple_of(i * model + first, step), size)]

    def give_copies(n):
        first, size = n % 2 * (model // 2), model // 2
        return [
            remote(
                given(i, first, size),
                taken(i, first, size),
                give_send.at[n, i],
                give_recv.at[n, i],
                at.sibling,
            )
            for i in ((0, 1) if n < 2 else (0,))
        ]

    def gate_out(n):
        slot = lax.rem(n, 2)
        return [
            pltpu.make_async_copy(
                grad_tile.at[slot, pl.ds(i * own_wide, own_wide)],
                ref.at[:, lanes_of(n)],
                grad_sem.at[slot, i],
            )
            for i, ref in enumerate((gate_grad_ref, up_grad_ref))
        ]

    def down_out(n):
        slot = lax.rem(n, 2)
        return pltpu.make_async_copy(
            grad_tile.at[slot, pl.ds(0, own_wide)],
            down_grad_ref.at[:, lanes_of(n)],
            grad_sem.at[slot, 0],
        )

    def reload(n):
        return pltpu.make_async_copy(
            cot_ref.at[:, lanes_of(n)], held.at[:, lanes_of(n)], reload_sem.at[n]
        )

    def gate_up_chunk(first, i, n):
        return jnp.dot(
            gate_up[turned_rows(i * wide + first)],
            held[:, lanes_of(n)],
            preferred_element_type=F32,
        )

    def down_chunk(first, n):
        return jnp.dot(
            down[turned_rows(first)], held[:, lanes_of(n)], preferred_element_type=F32
        )

    def in_half(n, body):
        half_chunks = chunks // 2
        pl.loop(n % 2 * half_chunks, (n % 2 + 1) * half_chunks)(body)

    for copy in turned:
        copy.wait()
    for part_of in (0, 1):

        def give_gate_up(n):
            for i in (0, 1):
                given(i, n * step, step)[...] = gate_up_chunk(theirs, i, n).astype(BF)

        in_half(part_of, give_gate_up)
        if part_of == 0:
            pl.semaphore_wait(give_ready, 1)
        for copy in give_copies(part_of):
            copy.start()

    reduce_own(2)
    for part_of in (0, 1):
        for copy in give_copies(part_of):
            copy.wait_recv()

        def own_gate_up(n):
            @pl.when(n >= 2)
            def _():
                for copy in gate_out(n):
                    copy.wait()

            for i in (0, 1):
                grad_tile[lax.rem(n, 2), i * own_wide : (i + 1) * own_wide] = gate_up_chunk(
                    mine, i, n
                ) + taken(i, n * step, step)[...].astype(F32)
            for copy in gate_out(n):
                copy.start()
            reload(n).start()

        in_half(part_of, own_gate_up)

    pl.semaphore_signal(give_ready, inc=1, device_id=at.sibling, device_id_type=MESH)
    reduce_x(3)
    reduce_y(3)
    pass_on(2)
    for part_of in (0, 1):
        for copy in give_copies(part_of):
            copy.wait_send()
    for part_of in (2, 3):

        def give_down(n):
            reload(n).wait()
            given(0, n * step, step)[...] = down_chunk(theirs, n).astype(BF)

        in_half(part_of, give_down)
        if part_of == 2:
            pl.semaphore_wait(give_ready, 1)
        for copy in give_copies(part_of):
            copy.start()

    for n in (0, 1):
        for copy in gate_out(n):
            copy.wait()
    for part_of in (2, 3):
        for copy in give_copies(part_of):
            copy.wait_recv()

        def own_down(n):
            @pl.when(n >= 2)
            def _():
                down_out(n).wait()

            grad_tile[lax.rem(n, 2), :own_wide] = down_chunk(mine, n) + taken(0, n * step, step)[
                ...
            ].astype(F32)
            down_out(n).start()

        in_half(part_of, own_down)

    reduce_own(3)
    for n in (0, 1):
        down_out(n).wait()

    for n in (2, 3):
        for copy in give_copies(n):
            copy.wait_send()
    for r in (2, 3):
        for copy in (half_a(r), half_b(r), x_copy(r), y_copy(r)):
            copy.wait_send()
    for r in (1, 2):

        @pl.when(inner)
        def _():
            far_copy(r).wait_send()

        @pl.when(jnp.logical_not(inner))
        def _():
            pair_copy(r).wait_send()


def experts_in_one(second_wide, cot_all, gate, up, down):
    rows, carried = second_wide.shape
    total_rows, model = cot_all.shape
    wide = 2 * down.shape[0]
    pair, half = 2 * rows, rows // 2
    both = 2 * model + EXTRA
    vmem = pl.BlockSpec(memory_space=pltpu.VMEM)
    hbm = pl.BlockSpec(memory_space=pl.ANY)
    dma = pltpu.SemaphoreType.DMA
    shape = jax.ShapeDtypeStruct
    return pl.pallas_call(
        expert_kernel,
        out_shape=(
            shape((rows, both), F32),
            shape((wide // 2, model), F32),
            shape((wide // 2, model), F32),
            shape((wide // 2, model), F32),
            shape((3 * wide, total_rows), BF),
        ),
        in_specs=[vmem, hbm, hbm, hbm, hbm],
        out_specs=(vmem, hbm, hbm, hbm, hbm),
        scratch_shapes=[
            pltpu.VMEM((total_rows, carried), BF),
            pltpu.VMEM((16 * rows, both), BF),
            pltpu.VMEM((2, half, both), BF),
            pltpu.VMEM((2, half, both), BF),
            pltpu.VMEM((rows, both), BF),
            pltpu.VMEM((2, rows, both), BF),
            pltpu.VMEM((2, rows, both), BF),
            pltpu.VMEM((2, rows, both), BF),
            pltpu.VMEM((2, rows, both), BF),
            pltpu.VMEM((pair, model), BF),
            pltpu.VMEM((2 * wide, model), BF),
            pltpu.VMEM((wide, model), BF),
            pltpu.VMEM((pair, 2 * wide), F32),
            pltpu.VMEM((pair, wide), F32),
            pltpu.VMEM((pair, 2 * wide), BF),
            pltpu.VMEM((pair, wide), BF),
            pltpu.VMEM((3 * wide, pair), BF),
            pltpu.VMEM((2, wide, 256), F32),
            pltpu.VMEM((EXTRA, wide), BF),
            pltpu.VMEM((wide, EXTRA), BF),
            dma((3,)),
            dma((3,)),
            dma((3,)),
            dma,
            dma,
            dma((2, 2)),
            dma((model // 256,)),
            dma((2,)),
            dma((4, 4)),
            dma((4, 4)),
            dma((3,)),
            dma((2,)),
            dma((2,)),
            dma((2,)),
            dma((4, 2)),
            dma((4, 2)),
            pltpu.SemaphoreType.REGULAR,
            *Line.semaphores(),
            *Gather.semaphores(False),
        ],
        compiler_params=pltpu.CompilerParams(
            collective_id=0, has_side_effects=True, vmem_limit_bytes=VMEM_BYTES
        ),
        cost_estimate=pl.CostEstimate(
            flops=2 * total_rows * model * wide * 9,
            bytes_accessed=8 * total_rows * model,
            transcendentals=total_rows * wide,
        ),
    )(second_wide, cot_all, gate, up, down)


def between(r, low, high):
    if isinstance(r, int):
        return low <= r <= high
    return (r >= low) & (r <= high)


class Tree:
    def __init__(self, at, refs, sems):
        (self.part, self.from_sib, self.diag_sum, self.x_sum, self.y_sum) = refs[:5]
        (self.diag_a, self.diag_b, self.x_whole, self.y_whole) = refs[5:]
        self.part_send, self.part_recv, self.send, self.recv = sems
        self.at = at
        self.rows = self.diag_sum.shape[0]
        self.half = self.rows // 2
        self.strip = 32

    def part_copy(self, q):
        return remote(
            self.part.at[q, 1 - self.at.core],
            self.from_sib.at[q],
            self.part_send.at[q],
            self.part_recv.at[q],
            self.at.sibling,
        )

    def half_a(self):
        there = self.diag_sum.at[pl.ds(0, self.half)]
        return remote(there, self.diag_a, self.send.at[0], self.recv.at[0], self.at.y_near)

    def half_b(self):
        there = self.diag_sum.at[pl.ds(self.half, self.half)]
        return remote(there, self.diag_b, self.send.at[1], self.recv.at[1], self.at.x_near)

    def x_copy(self):
        return remote(self.x_sum, self.x_whole, self.send.at[2], self.recv.at[2], self.at.x_near)

    def y_copy(self):
        return remote(self.y_sum, self.y_whole, self.send.at[3], self.recv.at[3], self.at.y_near)

    def strips(self, first, count, body):
        strip = self.strip

        @pl.loop(first // strip, (first + count) // strip)
        def _(i):
            body(pl.ds(pl.multiple_of(i * strip, strip), strip), i)

    def chip_sum(self, q, here):
        return self.part[q, self.at.core, here].astype(F32) + self.from_sib[q, here].astype(F32)

    def do_diag(self):
        self.part_copy(DIAG).wait_recv()

        def body(here, i):
            self.diag_sum[here] = self.chip_sum(DIAG, here).astype(BF)

        self.strips(0, self.rows, body)
        self.half_a().start()
        self.half_b().start()

    def do_x(self):
        self.part_copy(XCOL).wait_recv()
        self.half_a().wait_recv()

        def with_half(here, i):
            self.x_sum[here] = (
                self.chip_sum(XCOL, here) + self.diag_a[here].astype(F32)
            ).astype(BF)

        def alone(here, i):
            self.x_sum[here] = self.chip_sum(XCOL, here).astype(BF)

        self.strips(0, self.half, with_half)
        self.strips(self.half, self.half, alone)
        self.x_copy().start()

    def do_y(self):
        self.part_copy(YCOL).wait_recv()
        self.half_b().wait_recv()

        def alone(here, i):
            self.y_sum[here] = self.chip_sum(YCOL, here).astype(BF)

        def with_half(here, i):
            low = pl.ds(pl.multiple_of(i * self.strip - self.half, self.strip), self.strip)
            self.y_sum[here] = (self.chip_sum(YCOL, here) + self.diag_b[low].astype(F32)).astype(BF)

        self.strips(0, self.half, alone)
        self.strips(self.half, self.half, with_half)
        self.y_copy().start()

    def do_own(self, result):
        self.part_copy(OWN).wait_recv()
        self.x_copy().wait_recv()
        self.y_copy().wait_recv()

        def body(here, i):
            result[here] = (
                self.chip_sum(OWN, here)
                + self.x_whole[here].astype(F32)
                + self.y_whole[here].astype(F32)
            ).astype(BF)

        self.strips(0, self.rows, body)

    def drain(self):
        for q in range(4):
            self.part_copy(q).wait_send()
        for copy in (self.half_a(), self.half_b(), self.x_copy(), self.y_copy()):
            copy.wait_send()

    @staticmethod
    def buffers(rows, width):
        piece = pltpu.VMEM((rows, width), BF)
        half = pltpu.VMEM((rows // 2, width), BF)
        return [
            pltpu.VMEM((4, 2, rows, width), BF),
            pltpu.VMEM((4, rows, width), BF),
            piece,
            piece,
            piece,
            half,
            half,
            piece,
            piece,
        ]

    @staticmethod
    def semaphores():
        return [pltpu.SemaphoreType.DMA((4,))] * 4


class Spread:
    def __init__(self, at, own, out, sems, first=0):
        self.at, self.own, self.out, self.first = at, own, out, first
        self.send, self.recv, self.local = sems
        self.rows = own.shape[0]
        self.stride = out.shape[0] // 8
        self.e_x, self.e_y, self.e_d = at.x_near[0], at.y_near[0], at.diagonal

    def place(self, slot, first=0, rows=None):
        row = slot * self.stride + self.first + first
        rows = rows or self.rows
        return self.out.at[pl.ds(pl.multiple_of(row, rows), rows)]

    def to(self, src, slot, device, sem):
        return remote(src, self.place(slot), self.send.at[sem], self.recv.at[sem], device)

    def own_copies(self):
        e = self.at.e
        return (
            self.to(self.own, e, self.at.x_near, 0),
            self.to(self.own, e, self.at.y_near, 1),
            self.to(self.own, e, self.at.sibling, 2),
        )

    def here(self):
        return pltpu.make_async_copy(self.own, self.place(self.at.e), self.local)

    def half_copy(self, slot, first, device, sem):
        there = self.place(slot, first, self.rows // 2)
        return remote(there, there, self.send.at[sem], self.recv.at[sem], device)

    def cross_copies(self):
        return (
            self.half_copy(self.e_x, 0, self.at.y_near, 3),
            self.half_copy(self.e_y, self.rows // 2, self.at.x_near, 4),
            self.to(self.place(self.e_x), self.e_x, self.at.sibling, 5),
            self.to(self.place(self.e_y), self.e_y, self.at.sibling, 6),
        )

    def diag_copy(self):
        return self.to(self.place(self.e_d), self.e_d, self.at.sibling, 7)

    def begin(self):
        for copy in self.own_copies():
            copy.start()
        self.here().start()

    def cross(self):
        x, y, s = self.own_copies()
        x.wait_recv()
        y.wait_recv()
        for copy in self.cross_copies():
            copy.start()
        s.wait_recv()

    def diag(self):
        a, b, s, t = self.cross_copies()
        a.wait_recv()
        b.wait_recv()
        self.diag_copy().start()
        s.wait_recv()
        t.wait_recv()

    def end(self):
        self.diag_copy().wait()
        for copy in self.own_copies() + self.cross_copies():
            copy.wait_send()
        self.here().wait()

    @staticmethod
    def semaphores():
        dma = pltpu.SemaphoreType.DMA
        return [dma((8,)), dma((8,)), dma]


def swap(v):
    return pltpu.roll(v, v.shape[-1] // 2, v.ndim - 1)


def fold(v):
    return jnp.sum(v.reshape(v.shape[0] // 8, 8, v.shape[1]), axis=0)


def split_rows(v):
    high = v.astype(BF)
    return jnp.concatenate([v, v - high.astype(F32)], axis=0).astype(BF)


def back_kernel(
    middle_ref,
    share_ref,
    cot_ref,
    router_ref,
    small_ref,
    cos_ref,
    sin_ref,
    second_ref,
    place_ref,
    sums_ref,
    w_out_ref,
    w_cols_ref,
    mixed_ref,
    normed_ref,
    raw_ref,
    prob_ref,
    dnormed_ref,
    block_out_ref,
    middle_grad_ref,
    out_grad_ref,
    cols_grad_ref,
    w_out_held,
    w_cols_held,
    mixed_held,
    normed_held,
    raw_held,
    prob_held,
    held,
    raw_grad,
    left,
    right,
    share_sum,
    router_wide,
    rows_out,
    rows_in,
    gain_total,
    head_total,
    out_total,
    *rest,
):
    at = Place()
    rows, model = middle_ref.shape
    quarter = model // 4
    experts_all = router_ref.shape[1]
    own_part = dnormed_ref
    pair = 2 * rows
    width = HEAD_WIDTH
    heads = w_out_ref.shape[0] // width
    q_cols = heads * width
    cols = w_cols_ref.shape[1]
    count = model // 4 // 8
    scale = HEAD_WIDTH ** (-0.5)
    rest = list(rest)

    def grab(count):
        got, rest[:] = rest[:count], rest[count:]
        return got

    cols_totals, cols_alls = grab(2), grab(2)
    out_tree = Tree(at, grab(9), grab(4))
    cols_trees = [Tree(at, grab(9), grab(4)) for _ in (0, 1)]
    out_spread = Spread(at, out_total, out_grad_ref, grab(3))
    cols_spreads = [
        Spread(at, cols_alls[i], cols_grad_ref, grab(3), i * (count // 2)) for i in (0, 1)
    ]

    def line_block(b):
        return held.at[pl.ds(pl.multiple_of(b * rows, rows), rows)]

    line = Line(at, line_block, grab(2))
    sums = LineSum(at, rows_out, rows_in, grab(2))
    outer = (at.z == 0) | (at.z == 3)
    ex_send, ex_recv, ex_local, load_sem, sum_sem = grab(5)
    loads = [
        pltpu.make_async_copy(src, dst, load_sem.at[i])
        for i, (src, dst) in enumerate(
            (
                (w_out_ref, w_out_held),
                (raw_ref, raw_held),
                (w_cols_ref, w_cols_held),
                (normed_ref, normed_held),
                (prob_ref, prob_held),
                (mixed_ref, mixed_held),
            )
        )
    ]

    def sum_copy(j):
        lanes = pl.ds(pl.multiple_of(j * EXTRA, EXTRA), EXTRA)
        return pltpu.make_async_copy(sums_ref.at[:, lanes], prob_held.at[j], sum_sem.at[0])

    greet(at.everyone())
    columns = 2 * model // EXTRA
    share_copy = pltpu.make_async_copy(
        sums_ref.at[:, pl.ds(2 * model, EXTRA)], share_sum, sum_sem.at[1]
    )
    share_copy.start()

    @pl.loop(0, columns)
    def _(j):
        sum_copy(j).start()

    for copy in loads[:4]:
        copy.start()

    row_id = lax.broadcasted_iota(jnp.int32, right.shape, 0)
    lane_id = lax.broadcasted_iota(jnp.int32, right.shape, 1)
    chosen = (lane_id == experts_all) & (row_id >= rows) & (row_id < 2 * rows)
    for i in (0, 1, 2):
        first = 2 * rows + 16 * i
        chosen = chosen | (
            (lane_id == experts_all + 1 + i) & (row_id >= first) & (row_id < first + 16)
        )
    right[...] = chosen.astype(F32).astype(BF)
    router_wide[...] = jnp.zeros_like(router_wide)
    left[pl.ds(0, rows)] = second_ref[:, :model]
    left[pl.ds(2 * rows, rows)] = jnp.zeros((rows, model), BF)
    lane = lax.broadcasted_iota(jnp.int32, (rows, EXTRA), 1)
    share = share_ref[...]
    share_copy.wait()
    dshare = share_sum[...]
    dshare = dshare + pltpu.roll(dshare, EXTRA - experts_all, 1)
    weighed = jnp.where(lane < experts_all, share * dshare, 0.0)
    mean_share = jnp.sum(weighed, axis=-1, keepdims=True)
    logit_grad = jnp.where(lane < experts_all, share * (dshare - mean_share), 0.0).astype(BF)
    right[pl.ds(0, rows)] = logit_grad
    middle = middle_ref[...]
    inverse = lax.rsqrt(jnp.mean(middle * middle, axis=-1, keepdims=True) + epsilon)
    mean = jnp.zeros((rows, 1), F32)

    @pl.loop(0, columns)
    def _(j):
        sum_copy(j).wait()

    for j in range(4):
        router_wide[:experts_all, j * quarter : (j + 1) * quarter] = router_ref[j]
    for j in range(model // EXTRA):
        lanes = slice(j * EXTRA, (j + 1) * EXTRA)
        block_out_ref[:, lanes] = (middle[:, lanes] + prob_held[j]).astype(BF)
        second_grad = prob_held[model // EXTRA + j] + dot(logit_grad, router_wide[:, lanes], NN)
        unit = middle[:, lanes] * inverse
        left[rows : 2 * rows, lanes] = (second_grad * unit).astype(BF)
        of = j * EXTRA % quarter
        scaled = second_grad * small_ref[j * EXTRA // quarter, 1:2, of : of + EXTRA]
        middle_grad_ref[:, lanes] = scaled
        mean += jnp.sum(scaled * unit, axis=-1, keepdims=True)
    loads[4].start()
    loads[5].start()
    mean = mean / model
    middle_grad = cot_ref[...].astype(F32) + inverse * (
        middle_grad_ref[...] - middle * inverse * mean
    )
    middle_grad_ref[...] = middle_grad
    head_gains = small_ref[0, 2:3, :] + small_ref[1, 2:3, :]
    head_gains += small_ref[2, 2:3, :] + small_ref[3, 2:3, :]

    held[pl.ds(pl.multiple_of(at.z * rows, rows), rows)] = middle_grad.astype(BF)
    meet(at.everyone(), greeted=True)
    line.begin()
    gain_total[...] = jnp.zeros_like(gain_total)
    head_total[...] = jnp.zeros_like(head_total)

    def attention(far):
        first = 2 * (1 - at.half if far else at.half)
        both = pl.ds(pl.multiple_of(first * rows, pair), pair)
        mixed_grads = lax.dot_general(
            held[both, :], w_out_held[...], (NT, ((), ())), preferred_element_type=F32
        ).astype(BF)
        for i in (0, 1):
            heads_back(first + i, mixed_grads[i * rows : (i + 1) * rows])
            if not far and i == 0:

                @pl.when(jnp.logical_not(outer))
                def _():
                    line.arrive(3)

            if far and i == 0:
                out_tree.do_x()
                out_tree.do_y()
        step = 512
        for start in range(0, model, step):
            lanes = slice(start, start + step)
            part = lax.dot_general(
                raw_grad[both, :],
                w_cols_held[start : start + step, :],
                (NT, ((), ())),
                preferred_element_type=F32,
            )
            gain_total[:, lanes] += fold(part * normed_held[both, lanes].astype(F32))
            if not far:
                own_part[:, lanes] = jnp.where(at.z % 2 == 0, part[:rows], part[rows:])
            rows_out[first, :, lanes] = part[:rows].astype(BF)
            rows_out[first + 1, :, lanes] = part[rows:].astype(BF)
        if not far:
            sums.give_near(True)
        else:

            @pl.when(outer)
            def _():
                sums.give_far()

    def heads_back(b, mixed_grad):
        here = pl.ds(pl.multiple_of(b * rows, rows), rows)
        cosine, sine = cos_ref[here, :], sin_ref[here, :]

        def unit_of(v):
            inverse = lax.rsqrt(jnp.mean(v * v, axis=-1, keepdims=True) + epsilon)
            return v * inverse, inverse

        def low_of(unit, gain):
            scaled = unit * gain
            return (scaled * cosine + swap(scaled) * sine).astype(BF)

        def back_of(gradient, unit, inverse, gain, slot):
            turned = gradient * cosine - swap(gradient) * sine
            head_total[slot] += fold(turned * unit)
            return norm_back(turned * gain, unit, inverse).astype(BF)

        q_gain, k_gain = head_gains[:, :width], head_gains[:, width : 2 * width]
        k_unit, k_inverse = unit_of(raw_held[here, q_cols : q_cols + width])
        k_low = low_of(k_unit, k_gain)
        v_low = raw_held[here, q_cols + width : q_cols + 2 * width].astype(BF)
        k_grad = jnp.zeros((rows, width), F32)
        v_grad = jnp.zeros((rows, width), F32)
        for h in range(heads):
            lanes = slice(h * width, (h + 1) * width)
            q_unit, q_inverse = unit_of(raw_held[here, lanes])
            q_low = low_of(q_unit, q_gain)
            prob = prob_held[b * heads + h]
            own_grad = mixed_grad[:, lanes]
            v_grad += dot(prob.astype(BF), own_grad, TN)
            prob_grad = dot(own_grad, v_low, NT)
            score_grad = (
                prob * (prob_grad - jnp.sum(prob * prob_grad, axis=-1, keepdims=True))
            ).astype(BF)
            q_grad = dot(score_grad, k_low, NN) * scale
            k_grad += dot(score_grad, q_low, TN)
            raw_grad[here, lanes] = back_of(q_grad, q_unit, q_inverse, q_gain, 0)
        raw_grad[here, q_cols : q_cols + width] = back_of(
            k_grad * scale, k_unit, k_inverse, k_gain, 1
        )
        raw_grad[here, q_cols + width : q_cols + 2 * width] = v_grad.astype(BF)

    def out_piece(q):
        base = at.column_base(q)
        lanes = pl.ds(pl.multiple_of(base * width, 2 * width), 2 * width)
        left_side = mixed_held[:, lanes]
        step = 512
        for start in range(0, model, step):
            total = dot(left_side, held[:, start : start + step], TN)
            for c in (0, 1):
                out_tree.part[q, c, :, start : start + step] = total[
                    c * width : (c + 1) * width
                ].astype(BF)
        out_tree.part_copy(q).start()

    some = count // 2

    def cols_piece(q):
        base = at.column_base(q)
        for there in range(4):
            lanes = pl.ds(
                pl.multiple_of(there * (model // 4) + base * count, 2 * count), 2 * count
            )
            block = dot(normed_held[:, lanes], raw_grad[...], TN)
            small = dot(left[:, lanes], right[...], TN)
            for c in (0, 1):
                for i, tree in enumerate(cols_trees):
                    of = slice(c * count + i * some, c * count + (i + 1) * some)
                    here = pl.ds(there * some, some)
                    tree.part[q, c, here, :cols] = block[of].astype(BF)
                    tree.part[q, c, here, cols:] = small[of].astype(BF)
        cols_trees[0].part_copy(q).start()

    groups = ((0, q_cols), (q_cols, width), (q_cols + width, width), (cols, EXTRA))

    def exchange_refs(i, to, of):
        here = pl.ds(pl.multiple_of(to * some, some), some)
        first = 0
        refs = []
        for start, size in groups:
            lanes = pl.ds(pl.multiple_of(first + of * size, size), size)
            refs.append((cols_totals[i].at[here, pl.ds(start, size)], cols_alls[i].at[:, lanes]))
            first += 4 * size
        return refs

    def exchange(i, k):
        there = at.plane(k)
        turn = at.turn_at(there)
        return [
            remote(src, dst, ex_send.at[i, k - 1, j], ex_recv.at[i, turn - 1, j], (at.e, there))
            for j, (src, dst) in enumerate(exchange_refs(i, there, at.z))
        ]

    def exchange_arrival(i, k):
        return [
            remote(dst, dst, ex_send.at[i, k - 1, j], ex_recv.at[i, k - 1, j], at.sibling)
            for j, (src, dst) in enumerate(exchange_refs(i, at.z, at.plane(k)))
        ]

    def own_exchange(i):
        return [
            pltpu.make_async_copy(src, dst, ex_local.at[i, j])
            for j, (src, dst) in enumerate(exchange_refs(i, at.z, at.z))
        ]

    def begin_exchange(i):
        cols_trees[i].do_own(cols_totals[i])
        for k in (1, 2, 3):
            for copy in exchange(i, k):
                copy.start()
        for copy in own_exchange(i):
            copy.start()

    def end_exchange(i):
        for copy in own_exchange(i):
            copy.wait()
        for k in (1, 2, 3):
            for copy in exchange_arrival(i, k):
                copy.wait_recv()
        cols_spreads[i].begin()

    line.arrive(1)

    @pl.when(jnp.logical_not(outer))
    def _():
        line.arrive(2)

    for copy in loads[:5]:
        copy.wait()
    attention(False)

    @pl.when(outer)
    def _():
        line.arrive(2)
        line.arrive(3)

    loads[5].wait()
    for q in (DIAG, XCOL, YCOL, OWN):
        out_piece(q)
    out_tree.do_diag()
    attention(True)
    out_tree.do_own(out_total)
    out_spread.begin()
    for j in range(4):
        lanes = slice(j * quarter, (j + 1) * quarter)
        left[pl.ds(2 * rows, 16), lanes] = split_rows(
            gain_total[:, lanes] / small_ref[j, 0:1, :]
        )
    for slot in (0, 1):
        placed = jnp.dot(
            split_rows(head_total[slot]), place_ref[...], preferred_element_type=F32
        )
        left[pl.ds(2 * rows + 16 * (slot + 1), 16)] = placed.astype(BF)
    first, last = cols_trees
    for q in (DIAG, XCOL, YCOL, OWN):
        cols_piece(q)
    out_spread.cross()
    for q in (DIAG, XCOL, YCOL, OWN):
        last.part_copy(q).start()
    first.do_diag()
    last.do_diag()
    first.do_x()
    first.do_y()

    @pl.when(jnp.logical_not(outer))
    def _():
        sums.give_far()

    last.do_x()
    last.do_y()
    begin_exchange(0)
    sums.give_near(False)
    begin_exchange(1)
    end_exchange(0)
    out_spread.diag()
    end_exchange(1)
    cols_spreads[0].cross()
    sums.wait()

    @pl.loop(0, rows // 32)
    def _(i):
        here = pl.ds(pl.multiple_of(i * 32, 32), 32)
        dnormed_ref[here] += sums.total(here)

    cols_spreads[1].cross()
    cols_spreads[0].diag()
    cols_spreads[1].diag()
    out_spread.end()
    for spread in cols_spreads:
        spread.end()
    out_tree.drain()
    for tree in cols_trees:
        tree.drain()
    line.end()
    sums.end()
    for i in (0, 1):
        for k in (1, 2, 3):
            for copy in exchange(i, k):
                copy.wait_send()


def back_in_one(resident, sums, loaded):
    w_out, w_cols = loaded[:2]
    rows, model = resident[0].shape
    cols = w_cols.shape[1]
    wide = cols + EXTRA
    count = model // 4 // 8
    vmem = pl.BlockSpec(memory_space=pltpu.VMEM)
    hbm = pl.BlockSpec(memory_space=pl.ANY)
    dma = pltpu.SemaphoreType.DMA
    return pl.pallas_call(
        back_kernel,
        out_shape=(
            jax.ShapeDtypeStruct((rows, model), F32),
            jax.ShapeDtypeStruct((rows, model), BF),
            jax.ShapeDtypeStruct((rows, model), F32),
            jax.ShapeDtypeStruct((8 * HEAD_WIDTH, model), BF),
            jax.ShapeDtypeStruct((8 * count, 4 * wide), BF),
        ),
        in_specs=[vmem] * len(resident) + [hbm] * (1 + len(loaded)),
        out_specs=(vmem, vmem, vmem, hbm, hbm),
        scratch_shapes=[
            *[pltpu.VMEM(v.shape, v.dtype) for v in loaded],
            pltpu.VMEM((4 * rows, model), BF),
            pltpu.VMEM((4 * rows, cols), BF),
            pltpu.VMEM((3 * rows, model), BF),
            pltpu.VMEM((3 * rows, EXTRA), BF),
            pltpu.VMEM((rows, EXTRA), F32),
            pltpu.VMEM((EXTRA, model), BF),
            pltpu.VMEM((4, rows, model), BF),
            pltpu.VMEM((5, rows, model), BF),
            pltpu.VMEM((8, model), F32),
            pltpu.VMEM((2, 8, HEAD_WIDTH), F32),
            pltpu.VMEM((HEAD_WIDTH, model), BF),
            *[pltpu.VMEM((2 * count, wide), BF)] * 2,
            *[pltpu.VMEM((count // 2, 4 * wide), BF)] * 2,
            *Tree.buffers(HEAD_WIDTH, model),
            *Tree.semaphores(),
            *Tree.buffers(2 * count, wide),
            *Tree.semaphores(),
            *Tree.buffers(2 * count, wide),
            *Tree.semaphores(),
            *Spread.semaphores(),
            *Spread.semaphores(),
            *Spread.semaphores(),
            *Line.semaphores(),
            *LineSum.semaphores(),
            dma((2, 3, 4)),
            dma((2, 3, 4)),
            dma((2, 4)),
            dma((6,)),
            dma((2,)),
        ],
        compiler_params=pltpu.CompilerParams(
            collective_id=1, has_side_effects=True, vmem_limit_bytes=VMEM_BYTES
        ),
        cost_estimate=pl.CostEstimate(
            flops=2 * 4 * rows * model * cols * 5,
            bytes_accessed=64 * 1024 * 1024,
            transcendentals=4 * rows * cols,
        ),
    )(*resident, sums, *loaded)


def front_kernel(
    tokens_ref,
    small_ref,
    router_ref,
    w_query_ref,
    w_key_ref,
    w_value_ref,
    w_out_ref,
    table_ref,
    chosen_ref,
    cot_ref,
    second_ref,
    middle_ref,
    share_ref,
    w_cols_out,
    normed_out,
    raw_out,
    prob_out,
    mixed_out,
    cos_ref,
    sin_ref,
    small_all_ref,
    router_all_ref,
    cot_all_ref,
    w_cols_ref,
    normed_ref,
    raw_ref,
    prob_ref,
    mixed_ref,
    own_part,
    router_wide,
    rows_out,
    rows_in,
    small_send,
    small_recv,
    piece_send,
    piece_recv,
    piece_local,
    cot_local,
    store_sem,
    *sems,
):
    at = Place()
    rows, model = tokens_ref.shape
    pair = 2 * rows
    width = HEAD_WIDTH
    q_cols = w_query_ref.shape[1] // 4
    heads = q_cols // width
    cols = q_cols + 2 * width
    quarter = model // 4
    count = quarter // 8
    half = rows // 2
    experts_all = router_ref.shape[0]
    scale = HEAD_WIDTH ** (-0.5)
    meet(at.everyone())

    cot_here = pltpu.make_async_copy(cot_ref, cot_all_ref.at[at.z, at.e // 2], cot_local)
    cot_here.start()

    small_all_ref[at.z] = small_ref[...]
    router_all_ref[at.z] = router_ref[...]

    def small_copies(k):
        there = at.plane(k)
        turn = at.turn_at(there)
        return [
            remote(
                ref,
                ref_all.at[at.z],
                small_send.at[k - 1, i],
                small_recv.at[turn - 1, i],
                (at.e, there),
            )
            for i, (ref, ref_all) in enumerate(
                ((small_ref, small_all_ref), (router_ref, router_all_ref))
            )
        ]

    for k in (1, 2, 3):
        for copy in small_copies(k):
            copy.start()

    def w_block(k, q, i=None):
        first, size = (0, count) if i is None else (i * (count // 2), count // 2)
        row = at.plane(k) * quarter + at.own(q) * count + first
        return w_cols_ref.at[pl.ds(pl.multiple_of(row, count // 2), size)]

    def piece_refs(there):
        own = pl.ds(pl.multiple_of(at.e * count, count), count)
        row = pl.ds(pl.multiple_of(at.z * quarter + at.e * count, count), count)
        narrow = pl.ds(pl.multiple_of(there * width, width), width)
        return (
            (
                w_query_ref.at[own, pl.ds(pl.multiple_of(there * q_cols, q_cols), q_cols)],
                w_cols_ref.at[row, pl.ds(0, q_cols)],
            ),
            (w_key_ref.at[own, narrow], w_cols_ref.at[row, pl.ds(q_cols, width)]),
            (w_value_ref.at[own, narrow], w_cols_ref.at[row, pl.ds(q_cols + width, width)]),
        )

    def piece_copies(k):
        there = at.plane(k)
        turn = at.turn_at(there)
        return [
            remote(
                src, dst, piece_send.at[k - 1, i], piece_recv.at[turn - 1, i], (at.e, there)
            )
            for i, (src, dst) in enumerate(piece_refs(there))
        ]

    def pieces_arrive(k):
        block = w_block(k, OWN)
        for i, (first, size) in enumerate(((0, q_cols), (q_cols, width), (q_cols, width))):
            part = block.at[:, pl.ds(first, size)]
            remote(
                part, part, piece_send.at[k - 1, i], piece_recv.at[k - 1, i], at.sibling
            ).wait_recv()

    own_pieces = [
        pltpu.make_async_copy(src, dst, piece_local.at[i])
        for i, (src, dst) in enumerate(piece_refs(at.z))
    ]
    for copy in own_pieces:
        copy.start()
    for k in (1, 2, 3):
        for copy in piece_copies(k):
            copy.start()
    weights = Gather(at, w_block, sems[2:10])
    for copy in own_pieces:
        copy.wait()
    weights.own(0)

    def normed_block(b):
        return normed_ref.at[pl.ds(pl.multiple_of(b * rows, rows), rows)]

    line = Line(at, normed_block, sems[10:12])
    source = tokens_ref[...].astype(F32)
    inverse = lax.rsqrt(jnp.mean(source * source, axis=-1, keepdims=True) + epsilon)
    for k in (1, 2, 3):
        for i, ref_all in enumerate((small_all_ref, router_all_ref)):
            block = ref_all.at[at.plane(k)]
            remote(
                block, block, small_send.at[k - 1, i], small_recv.at[k - 1, i], at.sibling
            ).wait_recv()
    own_rows = pl.ds(pl.multiple_of(at.z * rows, rows), rows)
    for j in range(4):
        lanes = slice(j * quarter, (j + 1) * quarter)
        normed_ref[own_rows, lanes] = (source[:, lanes] * inverse * small_all_ref[j, 0:1, :]).astype(BF)
        router_wide[0:experts_all, lanes] = router_all_ref[j]
        router_wide[experts_all : 2 * experts_all, lanes] = router_all_ref[j]
    router_wide[2 * experts_all :] = jnp.zeros((EXTRA - 2 * experts_all, model), BF)
    line.begin()

    def cot_block(k, q, i=None):
        block = cot_all_ref.at[at.plane(k), at.column_base(q) // 2]
        return block if i is None else block.at[pl.ds(i * half, half)]

    def cot_line_block(b):
        return cot_all_ref.at[b, at.e // 2]

    cot_line = Line(at, cot_line_block, sems[12:14])
    cot_gather = Gather(at, cot_block, sems[14:], sibling=False)
    outer = (at.z == 0) | (at.z == 3)
    cot_here.wait()

    @pl.when(outer)
    def _():
        cot_line.begin()


    pieces_arrive(1)
    weights.own(1)
    line.arrive(1)
    pieces_arrive(2)
    weights.own(2)
    pieces_arrive(3)
    weights.own(3)

    @pl.when(jnp.logical_not(outer))
    def _():
        line.arrive(2)

    weights.cross(0)
    weights.cross(1)

    @pl.when(jnp.logical_not(outer))
    def _():
        line.arrive(3)
        cot_line.begin()

    cot_gather.own(0)
    weights.diag(0)
    weights.cross(2)
    weights.diag(1)
    weights.cross(3)
    weights.diag(2)
    weights.diag(3)
    stores = [
        pltpu.make_async_copy(src, dst, store_sem.at[i])
        for i, (src, dst) in enumerate(
            (
                (normed_ref, normed_out),
                (w_cols_ref, w_cols_out),
                (raw_ref, raw_out),
                (prob_ref, prob_out),
                (mixed_ref, mixed_out),
            )
        )
    ]
    for k in range(4):
        for q in range(4):
            weights.ready(k, q)
    stores[1].start()
    sums = LineSum(at, rows_out, rows_in, sems[:2])

    def project(far):
        first = 2 * (1 - at.half if far else at.half)
        both = pl.ds(pl.multiple_of(first * rows, pair), pair)
        step = 256
        for start in range(0, cols, step):
            lanes = slice(start, start + step)
            raw_ref[both, lanes] = jnp.dot(
                normed_ref[both, :], w_cols_ref[:, lanes], preferred_element_type=F32
            )

    gains = small_all_ref[0, 2:3, :] + small_all_ref[1, 2:3, :] + small_all_ref[2, 2:3, :] + small_all_ref[3, 2:3, :]
    q_gain, k_gain = gains[:, :width], gains[:, width : 2 * width]
    row_id = lax.broadcasted_iota(jnp.int32, (rows, rows), 0).astype(F32)
    lane_id = lax.broadcasted_iota(jnp.int32, (rows, rows), 1).astype(F32)

    def attention(far):
        first = 2 * (1 - at.half if far else at.half)
        both = pl.ds(pl.multiple_of(first * rows, pair), pair)
        for i in (0, 1):
            heads_of(first + i)
        step = 512
        for start in range(0, model, step):
            lanes = slice(start, start + step)
            part = jnp.dot(mixed_ref[both, :], w_out_ref[:, lanes], preferred_element_type=F32)
            if not far:
                own_part[:, lanes] = jnp.where(at.z % 2 == 0, part[:rows], part[rows:])
            rows_out[first, :, lanes] = part[:rows].astype(BF)
            rows_out[first + 1, :, lanes] = part[rows:].astype(BF)
        if far:
            sums.give_far()
        sums.give_near(not far)

    def heads_of(b):
        here = pl.ds(pl.multiple_of(b * rows, rows), rows)
        segment = jnp.zeros((rows, rows), F32)
        lane_segment = jnp.zeros((rows, rows), F32)
        place = row_id
        end = jnp.zeros((1, 1), F32)
        for i in range(SEQ_SLOTS - 1):
            length = small_all_ref[b, 2:3, 2 * width + i : 2 * width + i + 1]
            end = end + length
            past = (row_id >= end).astype(F32)
            segment += past
            place -= past * length
            lane_segment += (lane_id >= end).astype(F32)
        allowed = (segment == lane_segment) & (lane_id <= row_id)
        named = (lane_id == place).astype(BF)

        def looked_up(first):
            total = jnp.zeros((rows, width), F32)
            for i in range(3):
                part = table_ref[(first + i) * width : (first + i + 1) * width]
                total += jnp.dot(named, part, preferred_element_type=F32)
            return total

        cosine, sine = looked_up(0), looked_up(3)
        cos_ref[here, :] = cosine
        sin_ref[here, :] = sine

        def low_of(v, gain):
            inverse = lax.rsqrt(jnp.mean(v * v, axis=-1, keepdims=True) + epsilon)
            scaled = v * inverse * gain
            return (scaled * cosine + swap(scaled) * sine).astype(BF)

        k_low = low_of(raw_ref[here, q_cols : q_cols + width], k_gain)
        v_low = raw_ref[here, q_cols + width : q_cols + 2 * width].astype(BF)
        for h in range(heads):
            lanes = slice(h * width, (h + 1) * width)
            q_low = low_of(raw_ref[here, lanes], q_gain)
            scores = jnp.where(allowed, dot(q_low, k_low, NT) * scale, masked_score)
            weight = jnp.exp(scores - jnp.max(scores, axis=-1, keepdims=True))
            prob = weight / jnp.sum(weight, axis=-1, keepdims=True)
            prob_ref[b * heads + h] = prob
            mixed_ref[here, lanes] = dot(prob.astype(BF), v_low, NN).astype(BF)

    project(False)
    cot_line.arrive(1)
    cot_gather.own(1)
    attention(False)

    @pl.when(outer)
    def _():
        line.arrive(2)
        line.arrive(3)

    @pl.when(jnp.logical_not(outer))
    def _():
        cot_line.arrive(2)
        cot_gather.own(2)

    cot_gather.cross(0)
    stores[0].start()
    project(True)
    stores[2].start()

    @pl.when(jnp.logical_not(outer))
    def _():
        cot_line.arrive(3)
        cot_gather.own(3)

    cot_gather.cross(1)
    attention(True)
    stores[3].start()
    stores[4].start()

    @pl.when(outer)
    def _():
        cot_line.arrive(2)
        cot_gather.own(2)
        cot_line.arrive(3)
        cot_gather.own(3)

    cot_gather.diag(0)
    cot_gather.diag(1)
    cot_gather.cross(2)
    cot_gather.cross(3)
    sums.wait()
    middle = (
        tokens_ref[...].astype(F32)
        + own_part[...]
        + sums.total(pl.ds(0, rows))
    )
    middle_ref[...] = middle
    inverse = lax.rsqrt(jnp.mean(middle * middle, axis=-1, keepdims=True) + epsilon)
    for j in range(4):
        lanes = slice(j * quarter, (j + 1) * quarter)
        second_ref[:, lanes] = (middle[:, lanes] * inverse * small_all_ref[j, 1:2, :]).astype(BF)
    logits = dot(second_ref[:, :model], router_wide[...], NT)
    chosen = chosen_ref[...] > 0.0
    lane = lax.broadcasted_iota(jnp.int32, (rows, EXTRA), 1)
    top = jnp.max(jnp.where(chosen, logits, masked_score), axis=-1, keepdims=True)
    lifted = jnp.where(chosen, jnp.exp(logits - top), 0.0)
    share = lifted / jnp.sum(jnp.where(lane < experts_all, lifted, 0.0), axis=-1, keepdims=True)
    share_ref[...] = share
    high = share.astype(BF).astype(F32)
    second_ref[:, model:] = jnp.where(lane < experts_all, high, share - high).astype(BF)
    cot_gather.diag(2)
    cot_gather.diag(3)
    for copy in stores:
        copy.wait()
    for k in range(4):
        cot_gather.end(k)
        weights.end(k)
    line.end()
    cot_line.end()
    sums.end()
    for k in (1, 2, 3):
        for copy in small_copies(k):
            copy.wait_send()
        for copy in piece_copies(k):
            copy.wait_send()


def front_in_one(tokens, small, router, w_query, w_key, w_value, w_out, table, chosen, cotangent):
    rows, model = tokens.shape
    q_cols = w_query.shape[1] // 4
    cols = q_cols + 2 * HEAD_WIDTH
    heads = q_cols // HEAD_WIDTH
    experts_all = router.shape[0]
    vmem = pl.BlockSpec(memory_space=pltpu.VMEM)
    hbm = pl.BlockSpec(memory_space=pl.ANY)
    dma = pltpu.SemaphoreType.DMA
    shape = jax.ShapeDtypeStruct
    return pl.pallas_call(
        front_kernel,
        out_shape=(
            shape((rows, model + EXTRA), BF),
            shape((rows, model), F32),
            shape((rows, EXTRA), F32),
            shape((model, cols), BF),
            shape((4 * rows, model), BF),
            shape((4 * rows, cols), F32),
            shape((4 * heads, rows, rows), F32),
            shape((4 * rows, q_cols), BF),
            shape((4 * rows, HEAD_WIDTH), F32),
            shape((4 * rows, HEAD_WIDTH), F32),
            shape((4, 8, model // 4), F32),
            shape((4, experts_all, model // 4), BF),
            shape((4, 4, rows, model), BF),
        ),
        in_specs=[vmem, vmem, vmem, hbm, hbm, hbm, vmem, vmem, vmem, hbm],
        out_specs=(vmem,) * 3 + (hbm,) * 5 + (vmem,) * 4 + (hbm,),
        scratch_shapes=[
            pltpu.VMEM((model, cols), BF),
            pltpu.VMEM((4 * rows, model), BF),
            pltpu.VMEM((4 * rows, cols), F32),
            pltpu.VMEM((4 * heads, rows, rows), F32),
            pltpu.VMEM((4 * rows, q_cols), BF),
            pltpu.VMEM((rows, model), F32),
            pltpu.VMEM((EXTRA, model), BF),
            pltpu.VMEM((4, rows, model), BF),
            pltpu.VMEM((5, rows, model), BF),
            dma((3, 2)),
            dma((3, 2)),
            dma((3, 3)),
            dma((3, 3)),
            dma((3,)),
            dma,
            dma((5,)),
            *LineSum.semaphores(),
            *Gather.semaphores(),
            *Line.semaphores(),
            *Line.semaphores(),
            *Gather.semaphores(False),
        ],
        compiler_params=pltpu.CompilerParams(
            collective_id=2, has_side_effects=True, vmem_limit_bytes=VMEM_BYTES
        ),
        cost_estimate=pl.CostEstimate(
            flops=2 * 4 * rows * model * (cols + q_cols),
            bytes_accessed=64 * 1024 * 1024,
            transcendentals=4 * rows * cols,
        ),
    )(tokens, small, router, w_query, w_key, w_value, w_out, table, chosen, cotangent)


def per_device(
    tokens,
    lengths,
    routes,
    attn_gain,
    w_query,
    key_projection,
    value_projection,
    w_out,
    query_gain,
    key_gain,
    ffn_gain,
    w_router,
    w_gate,
    w_up,
    w_down,
    cotangent,
):
    ring = lax.axis_size("fsdp")
    groups = lax.axis_size("expert")
    plane_rank = lax.axis_index("expert")
    experts_all = w_router.shape[1]
    local_experts = w_gate.shape[0]
    units = w_gate.shape[2]
    wide = local_experts * units
    in_rows = MODEL_WIDTH // ring
    heads = QUERY_HEADS // ring
    kv = KEY_VALUE_HEADS // ring
    group_width = heads // kv
    q_cols = heads * HEAD_WIDTH
    kv_cols = kv * HEAD_WIDTH
    cols = q_cols + 2 * kv_cols
    piece_rows = in_rows // groups
    score_scale = HEAD_WIDTH ** (-0.5)
    both = ("expert", "fsdp")
    one_block = (groups, ring, experts_all) == (8, 4, 16)

    gate_w = w_gate.transpose(0, 2, 1).reshape(wide, MODEL_WIDTH)
    up_w = w_up.transpose(0, 2, 1).reshape(wide, MODEL_WIDTH)
    down_w = w_down.reshape(wide, MODEL_WIDTH)
    line_tokens = ring * DEVICE_TOKENS
    source = tokens.astype(F32)
    expert_ids = jnp.arange(experts_all, dtype=jnp.int32)
    chosen = jnp.any(routes[:, :, None] == expert_ids[None, None, :], axis=1)

    if one_block:
        here = lax.axis_index("fsdp") * (HEAD_WIDTH // ring)
        spread = lambda gain: lax.dynamic_update_slice_in_dim(
            jnp.zeros((HEAD_WIDTH,), F32), gain.astype(F32), here, 0
        )
        third = jnp.concatenate(
            [spread(query_gain), spread(key_gain), lengths.reshape(-1).astype(F32)]
        )
        small = jnp.stack(
            [
                attn_gain.astype(F32),
                ffn_gain.astype(F32),
                jnp.pad(third, (0, in_rows - third.shape[0])),
            ]
        )
        frequency = rope_base ** (-np.arange(0, HEAD_WIDTH, 2) / HEAD_WIDTH)
        angles = np.arange(HEAD_WIDTH)[:, None] * np.tile(frequency, 2)[None, :]
        sine_sign = np.where(np.arange(HEAD_WIDTH) < HEAD_WIDTH // 2, -1.0, 1.0)
        parts = []
        for exact in (np.cos(angles), np.sin(angles) * sine_sign):
            for _ in range(3):
                parts.append(exact.astype(ml_dtypes.bfloat16))
                exact = exact - parts[-1].astype(np.float64)
        wide_chosen = jnp.pad(
            jnp.concatenate([chosen, chosen], axis=1).astype(F32),
            ((0, 0), (0, EXTRA - 2 * experts_all)),
        )
        (
            second_wide,
            middle,
            share,
            w_cols,
            normed_all,
            raw,
            probabilities,
            mixed,
            cosine,
            sine_table,
            small_all,
            router_all,
            cot_all,
        ) = front_in_one(
            tokens,
            jnp.pad(small, ((0, 5), (0, 0))),
            w_router.T,
            w_query,
            key_projection,
            value_projection,
            w_out,
            jnp.asarray(np.concatenate(parts)),
            wide_chosen,
            cotangent,
        )
        cot_all = cot_all.reshape(-1, MODEL_WIDTH)
        attn_gain_f = small_all[:, 0].reshape(-1)
        attn_inverse = lax.rsqrt(jnp.mean(source * source, axis=-1, keepdims=True) + epsilon)
        attn_unit = source * attn_inverse
    else:
        small = jnp.concatenate(
            [
                attn_gain,
                ffn_gain,
                query_gain,
                key_gain,
                w_router.reshape(-1),
                lengths.reshape(-1).astype(BF),
            ]
        )
        small_all = lax.all_gather(small, "fsdp", axis=0, tiled=False)
        at = 0

        def take(count):
            nonlocal at
            part = small_all[:, at : at + count]
            at += count
            return part

        attn_gain_f = take(in_rows).reshape(-1).astype(F32)
        ffn_gain_f = take(in_rows).reshape(-1).astype(F32)
        query_gain_f = take(HEAD_WIDTH // ring).reshape(-1).astype(F32)
        key_gain_f = take(HEAD_WIDTH // ring).reshape(-1).astype(F32)
        router_all = take(in_rows * experts_all).reshape(MODEL_WIDTH, experts_all)
        lengths_all = take(SEQ_SLOTS).astype(jnp.int32)

        by_col = jnp.concatenate(
            [
                w_query.reshape(in_rows, ring, q_cols),
                key_projection.reshape(in_rows, ring, kv_cols),
                value_projection.reshape(in_rows, ring, kv_cols),
            ],
            axis=2,
        )
        piece = lax.dynamic_slice_in_dim(by_col, plane_rank * piece_rows, piece_rows, 0)
        piece = lax.all_to_all(
            piece.transpose(1, 0, 2), "fsdp", split_axis=0, concat_axis=0, tiled=True
        )
        w_cols = lax.all_gather(piece, "expert", axis=1, tiled=True).reshape(MODEL_WIDTH, cols)

        attn_inverse = lax.rsqrt(jnp.mean(source * source, axis=-1, keepdims=True) + epsilon)
        attn_unit = source * attn_inverse
        normed = (attn_unit * attn_gain_f).astype(BF)
        normed_all = lax.all_gather(normed, "fsdp", axis=0, tiled=True)
        raw = dot(normed_all, w_cols, NN)
        query_raw = raw[:, :q_cols].reshape(ring, DEVICE_TOKENS, kv, group_width, HEAD_WIDTH)
        key_raw = raw[:, q_cols : q_cols + kv_cols].reshape(ring, DEVICE_TOKENS, kv, HEAD_WIDTH)
        value_low = raw[:, q_cols + kv_cols :].astype(BF).reshape(ring, DEVICE_TOKENS, kv, HEAD_WIDTH)
        places, segment_ids = jax.vmap(lambda row: layout(row, DEVICE_TOKENS, SEQ_SLOTS))(lengths_all)
        cosine, sine_table = rope_tables(places, HEAD_WIDTH)
        cos_k, sin_k = cosine[:, :, None, :], sine_table[:, :, None, :]
        cos_q, sin_q = cosine[:, :, None, None, :], sine_table[:, :, None, None, :]
        query_inverse = lax.rsqrt(jnp.mean(query_raw * query_raw, axis=-1, keepdims=True) + epsilon)
        query_unit = query_raw * query_inverse
        query_low = rotate(query_unit * query_gain_f, cos_q, sin_q).astype(BF)
        key_inverse = lax.rsqrt(jnp.mean(key_raw * key_raw, axis=-1, keepdims=True) + epsilon)
        key_unit = key_raw * key_inverse
        key_low = rotate(key_unit * key_gain_f, cos_k, sin_k).astype(BF)
        row_ids = jnp.arange(DEVICE_TOKENS, dtype=jnp.int32)
        allowed = (segment_ids[:, :, None] == segment_ids[:, None, :]) & (
            row_ids[None, None, :] <= row_ids[None, :, None]
        )
        scores = (
            jnp.einsum("bqhgd,bkhd->bhgqk", query_low, key_low, preferred_element_type=F32)
            * score_scale
        )
        scores = jnp.where(allowed[:, None, None], scores, masked_score)
        weights = jnp.exp(scores - jnp.max(scores, axis=-1, keepdims=True))
        probabilities = weights / jnp.sum(weights, axis=-1, keepdims=True)
        prob_low = probabilities.astype(BF)
        mixed = (
            jnp.einsum("bhgqk,bkhd->bqhgd", prob_low, value_low, preferred_element_type=F32)
            .astype(BF)
            .reshape(line_tokens, q_cols)
        )
        branch = lax.psum_scatter(
            dot(mixed, w_out, NN).astype(BF), "fsdp", scatter_dimension=0, tiled=True
        ).astype(F32)
        middle = source + branch
        ffn_inverse = lax.rsqrt(jnp.mean(middle * middle, axis=-1, keepdims=True) + epsilon)
        ffn_unit = middle * ffn_inverse
        second = (ffn_unit * ffn_gain_f).astype(BF)

        logits = dot(second, router_all, NN)
        top = jnp.max(jnp.where(chosen, logits, -jnp.inf), axis=1, keepdims=True)
        lifted = jnp.where(chosen, jnp.exp(logits - top), 0.0)
        share = lifted / jnp.sum(lifted, axis=1, keepdims=True)

    def experts(second, share, cotangent):
        second_all = lax.all_gather(second, both, axis=0, tiled=True)
        share_all = lax.all_gather(share, both, axis=0, tiled=True)
        cot_all = lax.all_gather(cotangent, both, axis=0, tiled=True)
        first = plane_rank * local_experts
        own_share = lax.dynamic_slice_in_dim(share_all, first, local_experts, 1)
        share_wide = jnp.repeat(own_share, units, axis=1)
        gate_act = dot(second_all, gate_w, NT)
        up_act = dot(second_all, up_w, NT)
        back = dot(cot_all, down_w, NT)
        sigmoid_gate = jax.nn.sigmoid(gate_act)
        silu_gate = gate_act * sigmoid_gate
        hidden = silu_gate * up_act
        share_grad = jnp.sum((hidden * back).reshape(-1, local_experts, units), axis=2)
        hidden_low = (share_wide * hidden).astype(BF)
        hidden_grad = share_wide * back
        gate_grad = (
            hidden_grad * up_act * sigmoid_gate * (1.0 + gate_act * (1.0 - sigmoid_gate))
        ).astype(BF)
        up_grad = (hidden_grad * silu_gate).astype(BF)
        routed_part = dot(hidden_low, down_w, NN).astype(BF)
        second_part = (dot(gate_grad, gate_w, NN) + dot(up_grad, up_w, NN)).astype(BF)
        spread = jnp.zeros((share_grad.shape[0], experts_all), F32)
        spread = lax.dynamic_update_slice_in_dim(spread, share_grad, first, 1)
        second_grad = lax.psum_scatter(second_part, both, scatter_dimension=0, tiled=True)
        routed = lax.psum_scatter(routed_part, both, scatter_dimension=0, tiled=True)
        dshare = lax.psum_scatter(spread, both, scatter_dimension=0, tiled=True)
        return (
            (second_grad.astype(F32), routed.astype(F32), dshare),
            (
                dot(gate_grad, second_all, TN),
                dot(up_grad, second_all, TN),
                dot(hidden_low, cot_all, TN),
            ),
        )

    chunks = max(1, ring * groups // 32)
    if one_block:
        sums, *weight_grads, _ = experts_in_one(second_wide, cot_all, gate_w, up_w, down_w)
    elif chunks == 1:
        rows_out, weight_grads = experts(second, share, cotangent)
    else:
        def turn(total, rows):
            rows_out, grads = experts(*rows)
            return jax.tree.map(jnp.add, total, grads), rows_out

        start = (
            jnp.zeros((wide, MODEL_WIDTH), F32),
            jnp.zeros((wide, MODEL_WIDTH), F32),
            jnp.zeros((wide, MODEL_WIDTH), F32),
        )
        weight_grads, rows_out = lax.scan(
            turn,
            start,
            [v.reshape(chunks, -1, v.shape[1]) for v in (second, share, cotangent)],
        )
        rows_out = [v.reshape(-1, v.shape[2]) for v in rows_out]
    gate_wgrad, up_wgrad, down_wgrad = weight_grads
    grad_w_gate = gate_wgrad.reshape(local_experts, units, MODEL_WIDTH).transpose(0, 2, 1)
    grad_w_up = up_wgrad.reshape(local_experts, units, MODEL_WIDTH).transpose(0, 2, 1)
    grad_w_down = down_wgrad.reshape(local_experts, units, MODEL_WIDTH)
    if one_block:
        at_gain = experts_all
        part_width = HEAD_WIDTH // ring
        head_lane = np.arange(HEAD_WIDTH)
        place_of = head_lane // part_width * in_rows + head_lane % part_width
        placing = jnp.asarray(place_of[:, None] == np.arange(MODEL_WIDTH)[None, :], BF)
        normed_grad, block_out, middle_grad, out_sum, cols_sum = back_in_one(
            (
                middle,
                share,
                cotangent,
                router_all,
                small_all,
                cosine,
                sine_table,
                second_wide,
                placing,
            ),
            sums,
            (w_out, w_cols, mixed, normed_all, raw, probabilities),
        )
        tokens_grad = middle_grad + norm_back(normed_grad * attn_gain_f, attn_unit, attn_inverse)
        out_grad = out_sum.astype(F32)
        ends = [ring * n for n in (q_cols, q_cols + kv_cols, cols)]
        grad_w_query = cols_sum[:, : ends[0]].astype(F32)
        grad_w_key = cols_sum[:, ends[0] : ends[1]].astype(F32)
        grad_w_value = cols_sum[:, ends[1] : ends[2]].astype(F32)
        small_own = sum(
            cols_sum[:, ends[2] + j * EXTRA : ends[2] + (j + 1) * EXTRA].astype(F32)
            for j in range(ring)
        )
        own_grads = (
            small_own[:, at_gain + 1],
            small_own[:part_width, at_gain + 2],
            small_own[:part_width, at_gain + 3],
            small_own[:, at_gain],
            small_own[:, :experts_all],
        )
    else:
        second_grad, routed, dshare = rows_out
        block_out = (middle + routed).astype(BF)

        mean_grad = jnp.sum(share * dshare, axis=1, keepdims=True)
        logit_grad = (share * (dshare - mean_grad)).astype(BF)
        upstream = cotangent.astype(F32)
        second_grad = second_grad + dot(logit_grad, router_all, NT)
        middle_grad = upstream + norm_back(second_grad * ffn_gain_f, ffn_unit, ffn_inverse)
        router_grad = dot(second, logit_grad, TN)
        ffn_gain_grad = jnp.sum(second_grad * ffn_unit, axis=0)
        branch_all = lax.all_gather(middle_grad.astype(BF), "fsdp", axis=0, tiled=True)
        out_grad = lax.psum(dot(mixed, branch_all, TN).astype(BF), "expert").astype(F32)
        mixed_grad = dot(branch_all, w_out, NT).astype(BF)
        mixed_grad = mixed_grad.reshape(ring, DEVICE_TOKENS, kv, group_width, HEAD_WIDTH)
        value_grad = jnp.einsum("bhgqk,bqhgd->bkhd", prob_low, mixed_grad, preferred_element_type=F32)
        prob_grad = jnp.einsum("bqhgd,bkhd->bhgqk", mixed_grad, value_low, preferred_element_type=F32)
        score_grad = (
            probabilities * (prob_grad - jnp.sum(probabilities * prob_grad, axis=-1, keepdims=True))
        ).astype(BF)
        query_grad = (
            jnp.einsum("bhgqk,bkhd->bqhgd", score_grad, key_low, preferred_element_type=F32)
            * score_scale
        )
        key_grad = (
            jnp.einsum("bhgqk,bqhgd->bkhd", score_grad, query_low, preferred_element_type=F32)
            * score_scale
        )
        query_turned = unrotate(query_grad, cos_q, sin_q)
        query_gain_grad = jnp.sum(query_turned * query_unit, axis=(0, 1, 2, 3))
        query_back = norm_back(query_turned * query_gain_f, query_unit, query_inverse)
        key_turned = unrotate(key_grad, cos_k, sin_k)
        key_gain_grad = jnp.sum(key_turned * key_unit, axis=(0, 1, 2))
        key_back = norm_back(key_turned * key_gain_f, key_unit, key_inverse)
        raw_grad = jnp.concatenate(
            [
                query_back.astype(BF).reshape(line_tokens, q_cols),
                key_back.astype(BF).reshape(line_tokens, kv_cols),
                value_grad.astype(BF).reshape(line_tokens, kv_cols),
            ],
            axis=1,
        )
        cols_grad = dot(normed_all, raw_grad, TN).astype(BF)
        normed_part = dot(raw_grad, w_cols, NT).astype(BF)
        normed_grad = lax.psum_scatter(normed_part, "fsdp", scatter_dimension=0, tiled=True).astype(F32)
        attn_gain_grad = jnp.sum(normed_grad * attn_unit, axis=0)
        tokens_grad = middle_grad + norm_back(normed_grad * attn_gain_f, attn_unit, attn_inverse)

        own = lax.psum_scatter(
            cols_grad.reshape(ring, groups, piece_rows, cols), "expert", scatter_dimension=1, tiled=False
        )
        own = lax.all_to_all(own, "fsdp", split_axis=0, concat_axis=0, tiled=True)
        rows_grad = lax.all_gather(own, "expert", axis=1, tiled=True)
        rows_grad = rows_grad.transpose(1, 0, 2).astype(F32)
        grad_w_query = rows_grad[:, :, :q_cols].reshape(in_rows, QUERY_HEADS * HEAD_WIDTH)
        grad_w_key = rows_grad[:, :, q_cols : q_cols + kv_cols].reshape(in_rows, -1)
        grad_w_value = rows_grad[:, :, q_cols + kv_cols :].reshape(in_rows, -1)

        small_grad = jnp.concatenate(
            [
                attn_gain_grad.reshape(ring, -1),
                ffn_gain_grad.reshape(ring, -1),
                query_gain_grad.reshape(ring, -1),
                key_gain_grad.reshape(ring, -1),
                router_grad.reshape(ring, -1),
            ],
            axis=1,
        )
        small_own = lax.psum(small_grad, both)
        small_own = lax.dynamic_index_in_dim(small_own, lax.axis_index("fsdp"), 0, keepdims=False)
        a, b = in_rows, HEAD_WIDTH // ring
        own_grads = (
            small_own[:a],
            small_own[2 * a : 2 * a + b],
            small_own[2 * a + b : 2 * a + 2 * b],
            small_own[a : 2 * a],
            small_own[2 * a + 2 * b :].reshape(in_rows, experts_all),
        )
    return (
        block_out,
        tokens_grad,
        own_grads[0],
        grad_w_query,
        grad_w_key,
        grad_w_value,
        out_grad,
        own_grads[1],
        own_grads[2],
        own_grads[3],
        own_grads[4],
        grad_w_gate,
        grad_w_up,
        grad_w_down,
    )


def solution(mesh):
    rows = P(("expert", "fsdp"), None)
    return jax.shard_map(
        per_device,
        mesh=mesh,
        in_specs=(
            rows,
            rows,
            rows,
            P("fsdp"),
            P("fsdp", None),
            P("fsdp", None),
            P("fsdp", None),
            P("fsdp", None),
            P("fsdp"),
            P("fsdp"),
            P("fsdp"),
            P("fsdp", None),
            P("expert", None, "fsdp"),
            P("expert", None, "fsdp"),
            P("expert", "fsdp", None),
            rows,
        ),
        out_specs=(
            rows,
            rows,
            P("fsdp"),
            P("fsdp", None),
            P("fsdp", None),
            P("fsdp", None),
            P("fsdp", None),
            P("fsdp"),
            P("fsdp"),
            P("fsdp"),
            P("fsdp", None),
            P("expert", None, "fsdp"),
            P("expert", None, "fsdp"),
            P("expert", "fsdp", None),
        ),
        check_vma=False,
    )
```

time: 3460 us -> 554 us (0.16)
  waiting for transfers between devices: 2750 us -> 0 us
  Pallas kernels: 0 us -> 510 us
  blocking collectives: 237 us -> 0 us
  matrix products: 233 us -> 0 us
  local copies, waits for them, and re-layouts: 144 us -> 13.8 us
  other arithmetic: 65.5 us -> 20.3 us
    reduce_scatter x7 -> x0, waiting for transfers between devices: 1340 us -> none  [the longest x1 401 us: per_device(): lax.psum_scatter(partial_grad.astype(jnp.bfloat16), 'fsdp', scatter_dimen...]
    all_gather x6 -> x0, waiting for transfers between devices: 1280 us -> none  [the longest x1 392 us: per_device(): group_grad = lax.all_gather(arrived_grad, 'fsdp', axis=1, tiled=True)]
    pallas_call x0 -> x3, Pallas kernels: none -> 510 us  [the longest x1 239 us: experts_in_one(): pl.pallas_call(expert_kernel, out_shape=(shape((rows, both), F32), shape(...]
    dot_general x29 -> x0, matrix products: 230 us -> none  [the longest x1 26.5 us: per_device(): jnp.einsum('erf,edf->erd', up_grad_low, w_up, preferred_element_type=jnp....]
    all_to_all x2 -> x0, blocking collectives: 150 us -> none  [the longest x1 75.2 us: per_device(): lax.all_to_all(outgoing, 'expert', split_axis=0, concat_axis=2, tiled=True)]
    psum x1 -> x0, waiting for transfers between devices: 83.1 us -> none  [per_device(): lax.psum(owned[1].astype(jnp.bfloat16), 'expert').astype(jnp.float32)]
    gather x9 -> x0, local copies, waits for them, and re-layouts: 54.8 us -> none  [the longest x1 15.4 us: per_device(): padded_grad[owner_pair].reshape(groups, EXP_DEV, capacity, MODEL_WIDTH)]
    all_to_all x2 -> x0, waiting for transfers between devices: 45.2 us -> none  [the longest x1 45.2 us: per_device(): lax.all_to_all(rows_grad.reshape(1, EXP_DEV, groups * capacity, MODEL_WID...]
  transfers between devices with their start and end apart: 16 -> 0, of which waited for: 12 -> 0; matrix products, arithmetic and copies ran while one was open for 9% -> 0% of each run, Pallas kernels for 0% -> 0%
where the time goes in v1:
time: 554 us; the launch traced here: 545 us
  Pallas kernels  510 us (92%)
  other arithmetic  20.3 us (4%)
  local copies, waits for them, and re-layouts  13.8 us (2%)
    pallas_call x1, Pallas kernels, experts_in_one(): pl.pallas_call(expert_kernel, out_shape=(shape((rows, both), F32), shape(...  239 us
    pallas_call x1, Pallas kernels, back_in_one(): pl.pallas_call(back_kernel, out_shape=(jax.ShapeDtypeStruct((rows, model)...  138 us
    pallas_call x1, Pallas kernels, front_in_one(): pl.pallas_call(front_kernel, out_shape=(shape((rows, model + EXTRA), BF),...  133 us
    unnamed x17, local copies, waits for them, and re-layouts  11.2 us

profile of v1, /device:TPU:0, one launch (start us, length us, event | category | flops | bytes accessed | tf_op | source)
XLA Modules:
  0.0 545.0 jit_solution(6365666277305812635)
XLA Ops:
  0.7 0.8 convert_dynamic-update-slice_fusion.1
  1.4 0.7 convert_dynamic-update-slice_fusion
  2.2 0.7 convert_bitcast_fusion
  2.8 0.7 stack.24
  3.5 0.7 stack.25
  4.2 0.6 select_maximum_fusion.small_ref
  4.8 0.7 fusion.7
  5.5 0.1 copy.39
  5.6 0.6 pad_convert_fusion.chosen_ref
  6.3 133.1 %shard_map.281 = (bf16[128,2176]{1,0:T(8,128)(2,1)}, f32[128,2048]{1,0:T(8,128)}, f32[128,128]{1,0:T(8,128)}, bf16[2048,1280]{1,0:T(8,128)(2,1)}, bf16[512,2048]...) custom-call(bf16[128,2048]{1,0:T(8,128)(2,1)} %tokens_ref.1, ...), custom_call_target="tpu_custom_call" | custom-call | flops 4831838208 | bytes 67108864 | tf_op jit(solution)/shard_map/pallas_call | solution.py:2087
  139.4 238.5 %shard_map.282 = (f32[128,4224]{1,0:T(8,128)}, f32[384,2048]{1,0:T(8,128)}, f32[384,2048]{1,0:T(8,128)}, f32[384,2048]{1,0:T(8,128)}, bf16[2304,2048]{1,0:T(8,128)(2,1)}) custom-call(bf16[128,2176]{1,0:T(8,128)(2,1)} %get-tuple-element.42.second_ref, bf16[2048,2048]{1,0:T(8,128)(2,1)} %bitcast.36, bf16[384,2048]{1,0:T(8,128)(2,1)} %bitcast.32, ...), custom_call_target="tpu_custom_call" | custom-call | flops 57982058496 | bytes 33554432 | tf_op jit(solution)/shard_map/pallas_call | solution.py:961
  377.9 138.0 %shard_map.283 = (f32[128,2048]{1,0:T(8,128)}, bf16[128,2048]{1,0:T(8,128)(2,1)}, f32[128,2048]{1,0:T(8,128)}, bf16[1024,2048]{1,0:T(8,128)(2,1)}, bf16[512,5632]{1,0:T(8,128)(2,1)}) custom-call(f32[128,2048]{1,0:T(8,128)} %get-tuple-element.36.middle_ref, f32[128,128]{1,0:T(8,128)} %get-tuple-element.37.share_ref, bf16[128,2048]{1,0:T(8,128)(2,1)} %cot_ref.3, ...), custom_call_target="tpu_custom_call" | custom-call | flops 13421772800 | bytes 67108864 | tf_op jit(solution)/shard_map/pallas_call | solution.py:1655
  516.0 0.0 copy-start
  516.0 6.8 %convert_element_type.60 = f32[1024,2048]{1,0:T(8,128)} convert(bf16[1024,2048]{1,0:T(8,128)(2,1)} %get-tuple-element.54) | non-fusion elementwise | flops 2097152 | bytes 12582912 | tf_op jit(solution)/shard_map/convert_element_type | solution.py:2414
  522.8 0.0 copy-done
  522.8 0.0 copy-start.1
  522.8 4.5 slice_convert_fusion
  527.3 0.0 copy-start.2
  527.3 0.0 copy-start.5
  527.3 1.6 slice_convert_fusion.1
  528.9 0.8 slice.39
  529.8 0.0 copy-done.1
  529.8 0.2 fusion.6
  530.0 0.0 copy-done.2
  530.0 0.3 fusion.2
  530.3 0.0 copy-done.5
  530.3 1.4 fusion.5
  531.7 0.1 convert_add_fusion
  531.7 0.0 copy-start.4
  531.7 0.7 copy.40
  532.5 0.9 slice_reduce_fusion
  533.4 0.7 slice_reduce_fusion.2
  534.1 1.9 copy.47
  536.0 3.9 copy.48
  539.9 0.0 copy-done.4
  539.9 0.0 copy-start.3
  539.9 1.7 copy.49
  541.6 1.4 copy-done.3
  542.9 1.7 copy.50
  (6 shorter events, 0.0 us)
Async XLA Ops:
  516.0 6.8 %copy-start = (bf16[512,5632]{1,0:T(8,128)(2,1)S(1)}, bf16[512,5632]{1,0:T(8,128)(2,1)}, u32[]{:S(2)}) copy-start(bf16[512,5632]{1,0:T(8,128)(2,1)} %get-tuple-element.53) | copy-start | bytes 17301508
  522.8 7.0 %copy-start.1 = (bf16[128,2048]{1,0:T(8,128)(2,1)S(1)}, bf16[128,2048]{1,0:T(8,128)(2,1)}, u32[]{:S(2)}) copy-start(bf16[128,2048]{1,0:T(8,128)(2,1)} %tokens_ref.1) | copy-start | bytes 1572868
  527.3 2.7 copy-start.2
  527.3 3.0 copy-start.5
  531.7 8.2 %copy-start.4 = (f32[384,2048]{1,0:T(8,128)S(1)}, f32[384,2048]{1,0:T(8,128)}, u32[]{:S(2)}) copy-start(f32[384,2048]{1,0:T(8,128)} %get-tuple-element.56) | copy-start | bytes 9437188
  539.9 3.0 copy-start.3

commit v2 on v1

--- a/solution.py
+++ b/solution.py
@@ -1598,11 +1598,11 @@
     first, last = cols_trees
     for q in (DIAG, XCOL, YCOL, OWN):
         cols_piece(q)
-    out_spread.cross()
     for q in (DIAG, XCOL, YCOL, OWN):
         last.part_copy(q).start()
     first.do_diag()
     last.do_diag()
+    out_spread.cross()
     first.do_x()
     first.do_y()
 
@@ -1921,8 +1921,11 @@
     stores[1].start()
     sums = LineSum(at, rows_out, rows_in, sems[:2])
 
-    def project(far):
-        first = 2 * (1 - at.half if far else at.half)
+    def is_far(turn):
+        return outer if turn == 0 else jnp.logical_not(outer)
+
+    def project(turn):
+        first = 2 * jnp.where(is_far(turn), 1 - at.half, at.half)
         both = pl.ds(pl.multiple_of(first * rows, pair), pair)
         step = 256
         for start in range(0, cols, step):
@@ -1936,8 +1939,8 @@
     row_id = lax.broadcasted_iota(jnp.int32, (rows, rows), 0).astype(F32)
     lane_id = lax.broadcasted_iota(jnp.int32, (rows, rows), 1).astype(F32)
 
-    def attention(far):
-        first = 2 * (1 - at.half if far else at.half)
+    def attention(turn):
+        first = 2 * jnp.where(is_far(turn), 1 - at.half, at.half)
         both = pl.ds(pl.multiple_of(first * rows, pair), pair)
         for i in (0, 1):
             heads_of(first + i)
@@ -1945,13 +1948,21 @@
         for start in range(0, model, step):
             lanes = slice(start, start + step)
             part = jnp.dot(mixed_ref[both, :], w_out_ref[:, lanes], preferred_element_type=F32)
-            if not far:
+
+            @pl.when(jnp.logical_not(is_far(turn)))
+            def _():
                 own_part[:, lanes] = jnp.where(at.z % 2 == 0, part[:rows], part[rows:])
+
             rows_out[first, :, lanes] = part[:rows].astype(BF)
             rows_out[first + 1, :, lanes] = part[rows:].astype(BF)
-        if far:
+
+        @pl.when(is_far(turn))
+        def _():
             sums.give_far()
-        sums.give_near(not far)
+
+        if turn == 1:
+            sums.give_near(True)
+            sums.give_near(False)
 
     def heads_of(b):
         here = pl.ds(pl.multiple_of(b * rows, rows), rows)
@@ -1996,16 +2007,16 @@
             prob_ref[b * heads + h] = prob
             mixed_ref[here, lanes] = dot(prob.astype(BF), v_low, NN).astype(BF)
 
-    project(False)
-    cot_line.arrive(1)
-    cot_gather.own(1)
-    attention(False)
-
     @pl.when(outer)
     def _():
         line.arrive(2)
         line.arrive(3)
 
+    project(0)
+    cot_line.arrive(1)
+    cot_gather.own(1)
+    attention(0)
+
     @pl.when(jnp.logical_not(outer))
     def _():
         cot_line.arrive(2)
@@ -2013,7 +2024,7 @@
 
     cot_gather.cross(0)
     stores[0].start()
-    project(True)
+    project(1)
     stores[2].start()
 
     @pl.when(jnp.logical_not(outer))
@@ -2022,7 +2033,7 @@
         cot_gather.own(3)
 
     cot_gather.cross(1)
-    attention(True)
+    attention(1)
     stores[3].start()
     stores[4].start()
 

time: 554 us -> 544 us (0.982)
  Pallas kernels: 510 us -> 499 us
    pallas_call x1, Pallas kernels: 138 us -> 130 us  [back_in_one(): pl.pallas_call(back_kernel, out_shape=(jax.ShapeDtypeStruct((rows, model)...]
where the time goes in v2:
time: 544 us; the launch traced here: 535 us
  Pallas kernels  499 us (92%)
  other arithmetic  20.3 us (4%)
  local copies, waits for them, and re-layouts  13.8 us (3%)
    pallas_call x1, Pallas kernels, experts_in_one(): pl.pallas_call(expert_kernel, out_shape=(shape((rows, both), F32), shape(...  238 us
    pallas_call x1, Pallas kernels, front_in_one(): pl.pallas_call(front_kernel, out_shape=(shape((rows, model + EXTRA), BF),...  131 us
    pallas_call x1, Pallas kernels, back_in_one(): pl.pallas_call(back_kernel, out_shape=(jax.ShapeDtypeStruct((rows, model)...  130 us
    unnamed x17, local copies, waits for them, and re-layouts  11.2 us

profile of v2, /device:TPU:0, one launch (start us, length us, event | category | flops | bytes accessed | tf_op | source)
XLA Modules:
  0.0 534.7 jit_solution(17579487279797022671)
XLA Ops:
  0.7 0.8 convert_dynamic-update-slice_fusion.1
  1.4 0.7 convert_dynamic-update-slice_fusion
  2.2 0.7 convert_bitcast_fusion
  2.8 0.7 stack.24
  3.5 0.7 stack.25
  4.2 0.6 select_maximum_fusion.small_ref
  4.8 0.7 fusion.7
  5.5 0.1 copy.39
  5.6 0.6 pad_convert_fusion.chosen_ref
  6.3 131.2 %shard_map.281 = (bf16[128,2176]{1,0:T(8,128)(2,1)}, f32[128,2048]{1,0:T(8,128)}, f32[128,128]{1,0:T(8,128)}, bf16[2048,1280]{1,0:T(8,128)(2,1)}, bf16[512,2048]...) custom-call(bf16[128,2048]{1,0:T(8,128)(2,1)} %tokens_ref.1, ...), custom_call_target="tpu_custom_call" | custom-call | flops 4831838208 | bytes 67108864 | tf_op jit(solution)/shard_map/pallas_call | solution.py:2098
  137.5 238.0 %shard_map.282 = (f32[128,4224]{1,0:T(8,128)}, f32[384,2048]{1,0:T(8,128)}, f32[384,2048]{1,0:T(8,128)}, f32[384,2048]{1,0:T(8,128)}, bf16[2304,2048]{1,0:T(8,128)(2,1)}) custom-call(bf16[128,2176]{1,0:T(8,128)(2,1)} %get-tuple-element.42.second_ref, bf16[2048,2048]{1,0:T(8,128)(2,1)} %bitcast.36, bf16[384,2048]{1,0:T(8,128)(2,1)} %bitcast.32, ...), custom_call_target="tpu_custom_call" | custom-call | flops 57982058496 | bytes 33554432 | tf_op jit(solution)/shard_map/pallas_call | solution.py:961
  375.6 130.1 %shard_map.283 = (f32[128,2048]{1,0:T(8,128)}, bf16[128,2048]{1,0:T(8,128)(2,1)}, f32[128,2048]{1,0:T(8,128)}, bf16[1024,2048]{1,0:T(8,128)(2,1)}, bf16[512,5632]{1,0:T(8,128)(2,1)}) custom-call(f32[128,2048]{1,0:T(8,128)} %get-tuple-element.36.middle_ref, f32[128,128]{1,0:T(8,128)} %get-tuple-element.37.share_ref, bf16[128,2048]{1,0:T(8,128)(2,1)} %cot_ref.3, ...), custom_call_target="tpu_custom_call" | custom-call | flops 13421772800 | bytes 67108864 | tf_op jit(solution)/shard_map/pallas_call | solution.py:1655
  505.7 0.0 copy-start
  505.7 6.8 %convert_element_type.60 = f32[1024,2048]{1,0:T(8,128)} convert(bf16[1024,2048]{1,0:T(8,128)(2,1)} %get-tuple-element.54) | non-fusion elementwise | flops 2097152 | bytes 12582912 | tf_op jit(solution)/shard_map/convert_element_type | solution.py:2425
  512.5 0.0 copy-done
  512.5 0.0 copy-start.1
  512.5 4.5 slice_convert_fusion
  517.0 0.0 copy-start.2
  517.0 0.0 copy-start.5
  517.0 1.6 slice_convert_fusion.1
  518.6 0.8 slice.39
  519.5 0.0 copy-done.1
  519.5 0.2 fusion.6
  519.7 0.0 copy-done.2
  519.7 0.3 fusion.2
  520.0 0.0 copy-done.5
  520.0 1.4 fusion.5
  521.4 0.1 convert_add_fusion
  521.5 0.0 copy-start.4
  521.5 0.7 copy.40
  522.2 0.9 slice_reduce_fusion
  523.1 0.7 slice_reduce_fusion.2
  523.8 1.9 copy.47
  525.7 3.9 copy.48
  529.6 0.0 copy-done.4
  529.6 0.0 copy-start.3
  529.6 1.7 copy.49
  531.3 1.4 copy-done.3
  532.6 1.7 copy.50
  (6 shorter events, 0.0 us)
Async XLA Ops:
  505.7 6.8 %copy-start = (bf16[512,5632]{1,0:T(8,128)(2,1)S(1)}, bf16[512,5632]{1,0:T(8,128)(2,1)}, u32[]{:S(2)}) copy-start(bf16[512,5632]{1,0:T(8,128)(2,1)} %get-tuple-element.53) | copy-start | bytes 17301508
  512.5 7.0 %copy-start.1 = (bf16[128,2048]{1,0:T(8,128)(2,1)S(1)}, bf16[128,2048]{1,0:T(8,128)(2,1)}, u32[]{:S(2)}) copy-start(bf16[128,2048]{1,0:T(8,128)(2,1)} %tokens_ref.1) | copy-start | bytes 1572868
  517.0 2.7 copy-start.2
  517.0 3.0 copy-start.5
  521.5 8.2 %copy-start.4 = (f32[384,2048]{1,0:T(8,128)S(1)}, f32[384,2048]{1,0:T(8,128)}, u32[]{:S(2)}) copy-start(f32[384,2048]{1,0:T(8,128)} %get-tuple-element.56) | copy-start | bytes 9437188
  529.6 3.0 copy-start.3

commit v3 on v2

--- a/solution.py
+++ b/solution.py
@@ -880,9 +880,9 @@
                     copy.wait()
 
             for i in (0, 1):
-                grad_tile[lax.rem(n, 2), i * own_wide : (i + 1) * own_wide] = gate_up_chunk(
-                    mine, i, n
-                ) + taken(i, n * step, step)[...].astype(F32)
+                grad_tile[lax.rem(n, 2), i * own_wide : (i + 1) * own_wide] = (
+                    gate_up_chunk(mine, i, n) + taken(i, n * step, step)[...].astype(F32)
+                ).astype(BF)
             for copy in gate_out(n):
                 copy.start()
             reload(n).start()
@@ -920,9 +920,9 @@
             def _():
                 down_out(n).wait()
 
-            grad_tile[lax.rem(n, 2), :own_wide] = down_chunk(mine, n) + taken(0, n * step, step)[
-                ...
-            ].astype(F32)
+            grad_tile[lax.rem(n, 2), :own_wide] = (
+                down_chunk(mine, n) + taken(0, n * step, step)[...].astype(F32)
+            ).astype(BF)
             down_out(n).start()
 
         in_half(part_of, own_down)
@@ -962,9 +962,9 @@
         expert_kernel,
         out_shape=(
             shape((rows, both), F32),
-            shape((wide // 2, model), F32),
-            shape((wide // 2, model), F32),
-            shape((wide // 2, model), F32),
+            shape((wide // 2, model), BF),
+            shape((wide // 2, model), BF),
+            shape((wide // 2, model), BF),
             shape((3 * wide, total_rows), BF),
         ),
         in_specs=[vmem, hbm, hbm, hbm, hbm],
@@ -987,7 +987,7 @@
             pltpu.VMEM((pair, 2 * wide), BF),
             pltpu.VMEM((pair, wide), BF),
             pltpu.VMEM((3 * wide, pair), BF),
-            pltpu.VMEM((2, wide, 256), F32),
+            pltpu.VMEM((2, wide, 256), BF),
             pltpu.VMEM((EXTRA, wide), BF),
             pltpu.VMEM((wide, EXTRA), BF),
             dma((3,)),
@@ -1942,8 +1942,19 @@
     def attention(turn):
         first = 2 * jnp.where(is_far(turn), 1 - at.half, at.half)
         both = pl.ds(pl.multiple_of(first * rows, pair), pair)
-        for i in (0, 1):
-            heads_of(first + i)
+        heads_of(first)
+        if turn == 1:
+
+            @pl.when(outer)
+            def _():
+                cot_line.arrive(2)
+                cot_gather.own(2)
+
+            @pl.when(jnp.logical_not(outer))
+            def _():
+                cot_gather.cross(2)
+
+        heads_of(first + 1)
         step = 512
         for start in range(0, model, step):
             lanes = slice(start, start + step)
@@ -2039,14 +2050,12 @@
 
     @pl.when(outer)
     def _():
-        cot_line.arrive(2)
-        cot_gather.own(2)
         cot_line.arrive(3)
         cot_gather.own(3)
+        cot_gather.cross(2)
 
     cot_gather.diag(0)
     cot_gather.diag(1)
-    cot_gather.cross(2)
     cot_gather.cross(3)
     sums.wait()
     middle = (
@@ -2378,6 +2387,7 @@
     chunks = max(1, ring * groups // 32)
     if one_block:
         sums, *weight_grads, _ = experts_in_one(second_wide, cot_all, gate_w, up_w, down_w)
+        weight_grads = [grad.astype(F32) for grad in weight_grads]
     elif chunks == 1:
         rows_out, weight_grads = experts(second, share, cotangent)
     else:

time: 544 us -> 542 us (level)
  local copies, waits for them, and re-layouts: 13.8 us -> 4.15 us
  other arithmetic: 20.3 us -> 27.8 us
    unnamed x17 -> x14, local copies, waits for them, and re-layouts: 11.2 us -> 1.54 us
where the time goes in v3:
time: 542 us; the launch traced here: 532 us
  Pallas kernels  499 us (92%)
  other arithmetic  27.8 us (5%)
    pallas_call x1, Pallas kernels, experts_in_one(): pl.pallas_call(expert_kernel, out_shape=(shape((rows, both), F32), shape(...  238 us
    pallas_call x1, Pallas kernels, front_in_one(): pl.pallas_call(front_kernel, out_shape=(shape((rows, model + EXTRA), BF),...  131 us
    pallas_call x1, Pallas kernels, back_in_one(): pl.pallas_call(back_kernel, out_shape=(jax.ShapeDtypeStruct((rows, model)...  130 us

profile of v3, /device:TPU:0, one launch (start us, length us, event | category | flops | bytes accessed | tf_op | source)
XLA Modules:
  0.0 532.4 jit_solution(13608925873155488163)
XLA Ops:
  0.7 0.8 convert_dynamic-update-slice_fusion.1
  1.4 0.7 convert_dynamic-update-slice_fusion
  2.2 0.7 convert_bitcast_fusion.2
  2.8 0.7 stack.24
  3.5 0.7 stack.25
  4.2 0.6 select_maximum_fusion.small_ref
  4.8 0.7 fusion.7
  5.5 0.1 copy.39
  5.6 0.6 pad_convert_fusion.chosen_ref
  6.3 131.1 %shard_map.281 = (bf16[128,2176]{1,0:T(8,128)(2,1)}, f32[128,2048]{1,0:T(8,128)}, f32[128,128]{1,0:T(8,128)}, bf16[2048,1280]{1,0:T(8,128)(2,1)}, bf16[512,2048]...) custom-call(bf16[128,2048]{1,0:T(8,128)(2,1)} %tokens_ref.1, ...), custom_call_target="tpu_custom_call" | custom-call | flops 4831838208 | bytes 67108864 | tf_op jit(solution)/shard_map/pallas_call | solution.py:2107
  137.4 238.1 %shard_map.282 = (f32[128,4224]{1,0:T(8,128)}, bf16[384,2048]{1,0:T(8,128)(2,1)}, bf16[384,2048]{1,0:T(8,128)(2,1)}, bf16[384,2048]{1,0:T(8,128)(2,1)}, bf16[2304,2048]{1,0:T(8,128)(2,1)}) custom-call(bf16[128,2176]{1,0:T(8,128)(2,1)} %get-tuple-element.42.second_ref, bf16[2048,2048]{1,0:T(8,128)(2,1)} %bitcast.39, bf16[384,2048]{1,0:T(8,128)(2,1)} %bitcast.35, ...), custom_call_target="tpu_custom_call" | custom-call | flops 57982058496 | bytes 33554432 | tf_op jit(solution)/shard_map/pallas_call | solution.py:961
  375.5 5.4 %convert_bitcast_fusion = (f32[2,2048,192]{1,2,0:T(8,128)}, f32[2,2048,192]{1,2,0:T(8,128)}) fusion(bf16[2,192,2048]{2,1,0:T(8,128)(2,1)} %bitcast.28, bf16[2,192,2048]{2,1,0:T(8,128)(2,1)} %bitcast.27), kind=kLoop, calls=%fused_computation.1 | loop fusion | flops 1572864 | bytes 9437184 | tf_op jit(solution)/shard_map/transpose | solution.py:2411
  381.0 130.1 %shard_map.283 = (f32[128,2048]{1,0:T(8,128)}, bf16[128,2048]{1,0:T(8,128)(2,1)}, f32[128,2048]{1,0:T(8,128)}, bf16[1024,2048]{1,0:T(8,128)(2,1)}, bf16[512,5632]{1,0:T(8,128)(2,1)}) custom-call(f32[128,2048]{1,0:T(8,128)} %get-tuple-element.36.middle_ref, f32[128,128]{1,0:T(8,128)} %get-tuple-element.37.share_ref, bf16[128,2048]{1,0:T(8,128)(2,1)} %cot_ref.3, ...), custom_call_target="tpu_custom_call" | custom-call | flops 13421772800 | bytes 67108864 | tf_op jit(solution)/shard_map/pallas_call | solution.py:1655
  511.1 0.0 copy-start
  511.1 6.8 %convert_element_type.63 = f32[1024,2048]{1,0:T(8,128)} convert(bf16[1024,2048]{1,0:T(8,128)(2,1)} %get-tuple-element.54) | non-fusion elementwise | flops 2097152 | bytes 12582912 | tf_op jit(solution)/shard_map/convert_element_type | solution.py:2435
  517.9 0.0 copy-done
  517.9 4.5 slice_convert_fusion
  522.4 0.0 copy-start.1
  522.4 0.0 copy-start.2
  522.4 0.0 copy-start.4
  522.4 1.6 slice_convert_fusion.1
  524.0 0.8 slice.39
  524.8 0.0 copy-done.1
  524.8 0.2 fusion.6
  525.0 0.0 copy-done.2
  525.0 0.0 copy-start.3
  525.0 0.3 fusion.2
  525.4 0.0 copy-done.4
  525.4 1.4 fusion.5
  526.7 0.0 copy-start.5
  526.7 0.1 convert_add_fusion
  526.8 0.7 copy.40
  527.5 0.9 slice_reduce_fusion
  528.5 0.7 slice_reduce_fusion.2
  529.2 0.0 copy-done.3
  529.2 2.0 convert.11
  531.2 0.0 copy-done.5
  531.2 0.8 copy.44
  (6 shorter events, 0.0 us)
Async XLA Ops:
  511.1 6.8 %copy-start = (bf16[512,5632]{1,0:T(8,128)(2,1)S(1)}, bf16[512,5632]{1,0:T(8,128)(2,1)}, u32[]{:S(2)}) copy-start(bf16[512,5632]{1,0:T(8,128)(2,1)} %get-tuple-element.53) | copy-start | bytes 17301508
  522.4 2.5 copy-start.1
  522.4 2.7 copy-start.2
  522.4 3.0 copy-start.4
  525.0 4.1 copy-start.3
  526.7 4.5 copy-start.5

commit v4 on v3

--- a/solution.py
+++ b/solution.py
@@ -2203,20 +2203,31 @@
     chosen = jnp.any(routes[:, :, None] == expert_ids[None, None, :], axis=1)
 
     if one_block:
-        here = lax.axis_index("fsdp") * (HEAD_WIDTH // ring)
-        spread = lambda gain: lax.dynamic_update_slice_in_dim(
-            jnp.zeros((HEAD_WIDTH,), F32), gain.astype(F32), here, 0
-        )
-        third = jnp.concatenate(
-            [spread(query_gain), spread(key_gain), lengths.reshape(-1).astype(F32)]
-        )
-        small = jnp.stack(
-            [
-                attn_gain.astype(F32),
-                ffn_gain.astype(F32),
-                jnp.pad(third, (0, in_rows - third.shape[0])),
-            ]
-        )
+        quarter_of = jnp.arange(HEAD_WIDTH) // (HEAD_WIDTH // ring)
+        own_quarter = quarter_of == lax.axis_index("fsdp")
+
+        def spread(gain, first):
+            placed = jnp.where(own_quarter, jnp.tile(gain.astype(F32), ring), 0.0)
+            return jnp.pad(placed, (first, in_rows - first - HEAD_WIDTH))
+
+        first = 2 * HEAD_WIDTH
+        third = spread(query_gain, 0) + spread(key_gain, HEAD_WIDTH)
+        third += jnp.pad(
+            lengths.reshape(-1).astype(F32), (first, in_rows - first - SEQ_SLOTS)
+        )
+        row = jnp.arange(8)[:, None]
+        small = jnp.where(
+            row == 0,
+            attn_gain.astype(F32)[None, :],
+            jnp.where(
+                row == 1,
+                ffn_gain.astype(F32)[None, :],
+                jnp.where(row == 2, third[None, :], 0.0),
+            ),
+        )
+        lane = jnp.arange(EXTRA)
+        lane_expert = jnp.where(lane < 2 * experts_all, lane % experts_all, -1)
+        wide_chosen = jnp.any(routes[:, :, None] == lane_expert[None, None, :], axis=1).astype(F32)
         frequency = rope_base ** (-np.arange(0, HEAD_WIDTH, 2) / HEAD_WIDTH)
         angles = np.arange(HEAD_WIDTH)[:, None] * np.tile(frequency, 2)[None, :]
         sine_sign = np.where(np.arange(HEAD_WIDTH) < HEAD_WIDTH // 2, -1.0, 1.0)
@@ -2225,10 +2236,6 @@
             for _ in range(3):
                 parts.append(exact.astype(ml_dtypes.bfloat16))
                 exact = exact - parts[-1].astype(np.float64)
-        wide_chosen = jnp.pad(
-            jnp.concatenate([chosen, chosen], axis=1).astype(F32),
-            ((0, 0), (0, EXTRA - 2 * experts_all)),
-        )
         (
             second_wide,
             middle,
@@ -2245,7 +2252,7 @@
             cot_all,
         ) = front_in_one(
             tokens,
-            jnp.pad(small, ((0, 5), (0, 0))),
+            small,
             w_router.T,
             w_query,
             key_projection,

time: 542 us -> 540 us (level)
  no operation moved by 1% of the time
where the time goes in v4:
time: 540 us; the launch traced here: 531 us
  Pallas kernels  499 us (92%)
  other arithmetic  24.6 us (5%)
  local copies, waits for them, and re-layouts  6.31 us (1%)
    pallas_call x1, Pallas kernels, experts_in_one(): pl.pallas_call(expert_kernel, out_shape=(shape((rows, both), F32), shape(...  238 us
    pallas_call x1, Pallas kernels, front_in_one(): pl.pallas_call(front_kernel, out_shape=(shape((rows, model + EXTRA), BF),...  131 us
    pallas_call x1, Pallas kernels, back_in_one(): pl.pallas_call(back_kernel, out_shape=(jax.ShapeDtypeStruct((rows, model)...  130 us

profile of v4, /device:TPU:0, one launch (start us, length us, event | category | flops | bytes accessed | tf_op | source)
XLA Modules:
  0.0 531.4 jit_solution(9046311956273679272)
XLA Ops:
  0.6 0.7 tile.20
  1.3 0.1 tile.21
  1.4 0.7 tile.8
  2.0 0.1 tile.9
  2.1 0.7 convert_bitcast_fusion.2
  2.8 0.7 convert_element_type.57
  3.5 0.7 convert_element_type.58
  4.2 0.7 select_select_fusion.small_ref
  4.9 0.8 copy.36
  5.7 0.3 compare_reduce_fusion
  5.9 0.6 convert_element_type.63.chosen_ref
  6.6 131.1 %shard_map.281 = (bf16[128,2176]{1,0:T(8,128)(2,1)}, f32[128,2048]{1,0:T(8,128)}, f32[128,128]{1,0:T(8,128)}, bf16[2048,1280]{1,0:T(8,128)(2,1)}, bf16[512,2048]...) custom-call(bf16[128,2048]{1,0:T(8,128)(2,1)} %tokens_ref.1, ...), custom_call_target="tpu_custom_call" | custom-call | flops 4831838208 | bytes 67108864 | tf_op jit(solution)/shard_map/pallas_call | solution.py:2107
  137.7 238.1 %shard_map.282 = (f32[128,4224]{1,0:T(8,128)}, bf16[384,2048]{1,0:T(8,128)(2,1)}, bf16[384,2048]{1,0:T(8,128)(2,1)}, bf16[384,2048]{1,0:T(8,128)(2,1)}, bf16[2304,2048]{1,0:T(8,128)(2,1)}) custom-call(bf16[128,2176]{1,0:T(8,128)(2,1)} %get-tuple-element.42.second_ref, bf16[2048,2048]{1,0:T(8,128)(2,1)} %bitcast.33, bf16[384,2048]{1,0:T(8,128)(2,1)} %bitcast.29, ...), custom_call_target="tpu_custom_call" | custom-call | flops 57982058496 | bytes 33554432 | tf_op jit(solution)/shard_map/pallas_call | solution.py:961
  375.8 130.1 %shard_map.283 = (f32[128,2048]{1,0:T(8,128)}, bf16[128,2048]{1,0:T(8,128)(2,1)}, f32[128,2048]{1,0:T(8,128)}, bf16[1024,2048]{1,0:T(8,128)(2,1)}, bf16[512,5632]{1,0:T(8,128)(2,1)}) custom-call(f32[128,2048]{1,0:T(8,128)} %get-tuple-element.36.middle_ref, f32[128,128]{1,0:T(8,128)} %get-tuple-element.37.share_ref, bf16[128,2048]{1,0:T(8,128)(2,1)} %cot_ref.3, ...), custom_call_target="tpu_custom_call" | custom-call | flops 13421772800 | bytes 67108864 | tf_op jit(solution)/shard_map/pallas_call | solution.py:1655
  505.9 0.0 copy-start
  505.9 6.8 %convert_element_type.72 = f32[1024,2048]{1,0:T(8,128)} convert(bf16[1024,2048]{1,0:T(8,128)(2,1)} %get-tuple-element.54) | non-fusion elementwise | flops 2097152 | bytes 12582912 | tf_op jit(solution)/shard_map/convert_element_type | solution.py:2442
  512.7 0.0 copy-done
  512.7 4.5 slice_convert_fusion
  517.2 0.0 copy-start.1
  517.2 0.0 copy-start.2
  517.2 0.0 copy-start.6
  517.2 1.6 slice_convert_fusion.1
  518.8 0.8 slice.39
  519.7 0.0 copy-done.1
  519.7 0.2 fusion.6
  519.9 0.0 copy-done.2
  519.9 0.0 copy-start.5
  519.9 0.3 fusion.2
  520.2 0.0 copy-done.6
  520.2 1.4 fusion.5
  521.6 0.0 copy-start.4
  521.6 0.1 convert_add_fusion
  521.6 0.7 copy.37
  522.4 0.9 slice_reduce_fusion
  523.3 0.7 slice_reduce_fusion.2
  524.0 0.0 copy-done.5
  524.0 2.0 convert.7
  526.0 0.0 copy-start.3
  526.0 0.0 copy-done.4
  526.0 2.0 convert_bitcast_fusion
  528.1 0.0 copy-start.7
  528.1 0.0 copy-done.3
  528.1 2.0 convert_bitcast_fusion.1
  530.1 0.0 copy-done.7
  530.1 0.8 copy.39
  (7 shorter events, 0.0 us)
Async XLA Ops:
  505.9 6.8 %copy-start = (bf16[512,5632]{1,0:T(8,128)(2,1)S(1)}, bf16[512,5632]{1,0:T(8,128)(2,1)}, u32[]{:S(2)}) copy-start(bf16[512,5632]{1,0:T(8,128)(2,1)} %get-tuple-element.53) | copy-start | bytes 17301508
  517.2 2.5 copy-start.1
  517.2 2.7 copy-start.2
  517.2 3.0 copy-start.6
  519.9 4.1 copy-start.5
  521.6 4.5 copy-start.4
  526.0 2.0 copy-start.3
  528.1 2.0 copy-start.7
